TPU v7x, 256 devices: a whole 4x4x8 slice. The times are simulated.
256 devices in a mesh: lon: 16 (over y, x_lo, core), lat: 16 (over x_hi, z).
Axes of the slice: x: 4 (x_hi: 2, x_lo: 2; x = x_hi * 2 + x_lo), y: 4, z: 8, core: 2. Of those that a mesh axis runs over, the one named last changes fastest.
Arguments:
- state: float32 [16, 16, 256, 512], P('lon', 'lat'), may hold values from -6 to 6
- cotangent: float32 [16, 16, 256, 512], P('lon', 'lat'), may hold values from -6 to 6
- gains: float32 [2, 512], replicated, may hold values from -3 to 3
- senders: int32 [16, 16, 4, 4], P('lon', 'lat'), may hold values from 0 to 7
- halo_map: int32 [16, 16, 4, 1], P('lon', 'lat'), may hold values from 0 to 3
- edge_in: bfloat16 [2, 1024, 512], replicated, may hold values from -0.1875 to 0.1875
- edge_out: bfloat16 [2, 512, 512], replicated, may hold values from -0.25 to 0.25
- node_in: bfloat16 [2, 1024, 512], replicated, may hold values from -0.1875 to 0.1875
- node_out: bfloat16 [2, 512, 512], replicated, may hold values from -0.25 to 0.25
Outputs:
- result: float32 [16, 16, 256, 512], P('lon', 'lat')
- grad_state: float32 [16, 16, 256, 512], P('lon', 'lat')
- grad_gains: float32 [2, 512], replicated
All inputs are finite; a program needn't handle non-finite values.
Results may differ from a plain program's by a relative error of at most 0.025.
Values may be sent and summed in bfloat16 or wider, within the bound.
A program may use at most 64 MiB of HBM per device.

v0:
```python
from functools import partial

import jax
import jax.numpy as jnp
from jax import lax
from jax.sharding import PartitionSpec as P


def padded(cells, sides, width, closed):
    for axis, dim in sides:
        count = lax.axis_size(axis)
        ends = count if closed else count - 1
        head = lax.slice_in_dim(cells, 0, width, axis=dim)
        tail = lax.slice_in_dim(cells, cells.shape[dim] - width, cells.shape[dim], axis=dim)
        cells = jnp.concatenate(
            [
                lax.ppermute(tail, axis, [(i, (i + 1) % count) for i in range(ends)]),
                cells,
                lax.ppermute(head, axis, [((i + 1) % count, i) for i in range(ends)]),
            ],
            axis=dim,
        )
    return cells


def rms_scale(rows, gain):
    mean_sq = jnp.mean(rows * rows, axis=-1, keepdims=True)
    return (rows * jax.lax.rsqrt(mean_sq + 1e-06) * (1.0 + gain)).astype(jnp.bfloat16)


def local(state, cotangent, gains, senders, halo_map, edge_in, edge_out, node_in, node_out):
    nblk, slots = (senders.shape[2], senders.shape[3])
    nodes, width = (state.shape[2], state.shape[3])
    block = nodes // nblk
    halo_blocks = halo_map.shape[3]
    layers = gains.shape[0]
    picks = halo_map.reshape(4 * halo_blocks)
    links = senders.reshape(nblk * slots)

    def prepare(current, gain):
        normed = rms_scale(current, gain)
        outgoing = jnp.take(current, picks, axis=0)
        lon_pair = jnp.stack([outgoing[1], outgoing[0]])
        lat_pair = jnp.stack([outgoing[3], outgoing[2]])
        return (normed, lon_pair, lat_pair)

    def combine(current, normed, pieces, gain, first_edge, second_edge, first_node, second_node):
        received = jnp.stack(pieces)
        received = rms_scale(received, gain)
        sources = jnp.concatenate([normed, received], axis=0)
        project_src = jnp.dot(sources, first_edge[:width], preferred_element_type=jnp.float32)
        project_dst = jnp.dot(normed, first_edge[width:], preferred_element_type=jnp.float32)
        chosen = jnp.take(project_src, links, axis=0).reshape(nblk, slots, block, width)
        edges = jax.nn.silu(chosen + project_dst[:, None]).astype(jnp.bfloat16)
        messages = jnp.dot(edges, second_edge, preferred_element_type=jnp.float32)
        total = jnp.sum(messages, axis=1).astype(jnp.bfloat16)
        inner = jnp.dot(normed, first_node[:width], preferred_element_type=jnp.float32)
        inner = inner + jnp.dot(total, first_node[width:], preferred_element_type=jnp.float32)
        hidden = jax.nn.silu(inner).astype(jnp.bfloat16)
        return current + jnp.dot(hidden, second_node, preferred_element_type=jnp.float32)

    current = state.reshape(nblk, block, width)
    undo_list = []
    for layer in range(layers):
        gain = gains[layer]
        (normed, lon_pair, lat_pair), undo_prep = jax.vjp(prepare, current, gain)
        trade_lon_wide = padded(lon_pair.astype(jnp.bfloat16), (("lon", 0),), 1, True).astype(
            lon_pair.dtype
        )
        trade_lat_wide = padded(lat_pair.astype(jnp.bfloat16), (("lat", 0),), 1, False).astype(
            lat_pair.dtype
        )
        pieces = (trade_lon_wide[0], trade_lon_wide[3], trade_lat_wide[0], trade_lat_wide[3])
        stepper = partial(
            combine,
            first_edge=edge_in[layer],
            second_edge=edge_out[layer],
            first_node=node_in[layer],
            second_node=node_out[layer],
        )
        current, undo_comb = jax.vjp(stepper, current, normed, pieces, gain)
        undo_list.append((undo_prep, undo_comb, lon_pair.dtype))
    grad = cotangent.reshape(nblk, block, width)
    gain_terms = [None] * layers
    for layer in reversed(range(layers)):
        undo_prep, undo_comb, wire_type = undo_list[layer]
        grad_cur, grad_norm, grad_pieces, grad_gain = undo_comb(grad)
        lon_grads = jnp.stack([grad_pieces[0], grad_pieces[1]])
        lat_grads = jnp.stack([grad_pieces[2], grad_pieces[3]])
        lon_wide = padded(lon_grads.astype(jnp.bfloat16), (("lon", 0),), 1, True).astype(
            lon_grads.dtype
        )
        lat_wide = padded(lat_grads.astype(jnp.bfloat16), (("lat", 0),), 1, False).astype(
            lat_grads.dtype
        )
        lon_back = jnp.stack([lon_wide[0], lon_wide[3]])
        lat_back = jnp.stack([lat_wide[0], lat_wide[3]])
        grad_more, gain_more = undo_prep((grad_norm, lon_back, lat_back))
        grad = grad_cur + grad_more
        gain_terms[layer] = grad_gain + gain_more
    grad_gains = lax.psum(jnp.stack(gain_terms), ("lon", "lat"))
    return (current.reshape(1, 1, nodes, width), grad.reshape(1, 1, nodes, width), grad_gains)


def solution(mesh):
    in_specs = (
        P("lon", "lat", None, None),
        P("lon", "lat", None, None),
        P(),
        P("lon", "lat", None, None),
        P("lon", "lat", None, None),
        P(),
        P(),
        P(),
        P(),
    )
    out_specs = (P("lon", "lat", None, None), P("lon", "lat", None, None), P())
    return jax.shard_map(local, mesh=mesh, in_specs=in_specs, out_specs=out_specs, check_vma=False)
```

profile of v0, /device:TPU:1, one launch (start us, length us, event | category | flops | bytes accessed | tf_op | source)
XLA Modules:
  0.0 198.9 jit_solution(12379657045954930405)
XLA Ops:
  2.2 1.6 gather_fusion
  4.0 2.7 %collective-permute-start = (bf16[1,64,512]{2,1,0:T(8,128)(2,1)S(1)}, bf16[1,64,512]{2,1,0:T(8,128)(2,1)S(1)}, u32[]{:S(2)}, u32[]{:S(2)}) collective-permute-start(bf16[1,64,512]{2,1,0:T(8,128)(2,1)S(1)} %get-tuple-element.61), channel_id=1, source_target_pairs={{0,16},{16,32},{32,48},{48,64},{64,80},{80,96},{96,112},{112,128},... | collective-permute-start | bytes 196616 | tf_op jit(solution)/shard_map/ppermute | solution.py:17
  7.4 3.4 %collective-permute-start.2 = (bf16[1,64,512]{2,1,0:T(8,128)(2,1)S(1)}, bf16[1,64,512]{2,1,0:T(8,128)(2,1)}, u32[]{:S(2)}, u32[]{:S(2)}) collective-permute-start(bf16[1,64,512]{2,1,0:T(8,128)(2,1)S(1)} %get-tuple-element.63), channel_id=1, source_target_pairs={{0,1},{1,2},{2,3},{3,4},{4,5},{5,6},{6,7},{7,8},{8,9},{9,10},{10,1... | collective-permute-start | bytes 196616 | tf_op jit(solution)/shard_map/ppermute | solution.py:17
  10.8 1.3 collective-permute-start.3
  12.1 1.2 multiply_reduce_fusion.7
  15.0 2.3 %fusion.66 = f32[4,64,512]{2,1,0:T(8,128)} fusion(bf16[4,64,512]{2,1,0:T(8,128)(2,1)S(1)} %bitcast.147, bf16[2,1024,512]{2,1,0:T(8,128)(2,1)} %param.20), kind=kOutput, calls=%fused_computation.116 | convolution fusion | flops 134217728 | bytes 1310720 | tf_op jit(solution)/shard_map/jvp()/dot_general | solution.py:57
  18.6 0.9 maximum_convert_fusion.7
  19.5 0.9 maximum_convert_fusion.6
  21.2 1.4 fusion.32
  22.6 2.0 %gather_fusion.1 = f32[16,64,512]{2,1,0:T(8,128)S(1)} fusion(f32[8,64,512]{2,1,0:T(8,128)} %fusion.32, s32[1024]{0:T(1024)} %pad_clamp_fusion), kind=kCustom, calls=%fused_computation.1.clone | custom fusion | bytes 4194368 | tf_op jit(solution)/shard_map/jvp(jit(_take))/gather | solution.py:53
  24.7 2.1 %multiply_convert_fusion.1 = (bf16[16,64,512]{2,1,0:T(8,128)(2,1)S(1)}, f32[16,64,512]{2,1,0:T(8,128)}) fusion(f32[4,64,512]{2,1,0:T(8,128)S(1)} %fusion.61, f32[16,64,512]{2,1,0:T(8,128)S(1)} %gather_fusion.1, pred[16]{0:T(512)(128)(4,1)S(1)} %copy-done.51), kind=kLoop, calls=%fused_computation.21 | loop fusion | flops 3670016 | bytes 5767184 | tf_op jit(solution)/shard_map/jvp()/convert_element_type | solution.py:54
  27.5 0.9 copy-done.2
  30.0 1.4 gather_fusion.2
  31.4 1.2 select_convert_fusion
  32.7 2.1 %collective-permute-start.4 = (bf16[1,64,512]{2,1,0:T(8,128)(2,1)S(1)}, bf16[1,64,512]{2,1,0:T(8,128)(2,1)S(1)}, u32[]{:S(2)}, u32[]{:S(2)}) collective-permute-start(bf16[1,64,512]{2,1,0:T(8,128)(2,1)S(1)} %get-tuple-element.53), channel_id=1, source_target_pairs={{0,16},{16,32},{32,48},{48,64},{64,80},{80,96},{96,112},{112,128},... | collective-permute-start | bytes 196616 | tf_op jit(solution)/shard_map/ppermute | solution.py:17
  34.8 1.1 collective-permute-start.5
  35.9 4.3 %collective-permute-start.6 = (bf16[1,64,512]{2,1,0:T(8,128)(2,1)S(1)}, bf16[1,64,512]{2,1,0:T(8,128)(2,1)S(1)}, u32[]{:S(2)}, u32[]{:S(2)}) collective-permute-start(bf16[1,64,512]{2,1,0:T(8,128)(2,1)S(1)} %get-tuple-element.55), channel_id=1, source_target_pairs={{0,1},{1,2},{2,3},{3,4},{4,5},{5,6},{6,7},{7,8},{8,9},{9,10},{10,1... | collective-permute-start | bytes 196616 | tf_op jit(solution)/shard_map/ppermute | solution.py:17
  40.2 1.5 collective-permute-start.7
  41.7 3.4 %collective-permute-done.7 = bf16[1,64,512]{2,1,0:T(8,128)(2,1)S(1)} collective-permute-done((bf16[1,64,512]{2,1,0:T(8,128)(2,1)S(1)}, bf16[1,64,512]{2,1,0:T(8,128)(2,1)S(1)}, u32[]{:S(2)}, u32[]{:S(2)}) %collective-permute-start.7) | collective-permute-done | bytes 65568 | tf_op jit(solution)/shard_map/ppermute | solution.py:19
  46.2 1.1 fusion.49
  47.3 1.1 fusion.54
  48.4 1.4 fusion.36
  49.8 2.0 %gather_fusion.3 = f32[16,64,512]{2,1,0:T(8,128)S(1)} fusion(f32[8,64,512]{2,1,0:T(8,128)} %fusion.36, s32[1024]{0:T(1024)} %pad_clamp_fusion), kind=kCustom, calls=%fused_computation.3.clone | custom fusion | bytes 4194368 | tf_op jit(solution)/shard_map/jvp(jit(_take))/gather | solution.py:53
  51.9 2.0 multiply_convert_fusion
  55.9 1.1 convolution_add_fusion
  58.1 3.4 %fusion.122 = (bf16[4,64,512]{2,1,0:T(8,128)(2,1)}, f32[4,4,64,512]{3,2,1,0:T(8,128)}) fusion(f32[4,4,64,512]{3,2,1,0:T(8,128)S(1)} %bitcast.149, f32[4,64,512]{2,1,0:T(8,128)S(1)} %copy-done.7, bf16[2,512,512]{2,1,0:T(8,128)(2,1)S(1)} %copy-done.57, bf16[4,64,512]{2,1,0:T(8,128)(2,1)S(1)} %fusion.6), kind=kOutput, calls=%fused_computation.234 | convolution fusion | flops 543031296 | bytes 5767168 | tf_op jit(solution)/shard_map/transpose(jvp())/dot_general | solution.py:55
  61.6 3.5 %scatter_fusion = f32[8,64,512]{2,1,0:T(8,128)S(1)} fusion(f32[8,64,512]{2,1,0:T(8,128)S(1)} %broadcast_in_dim.55.clone, s32[16]{0:T(128)S(1)} %copy-done.48, f32[16,64,512]{2,1,0:T(8,128)} %bitcast.151), kind=kCustom, calls=%fused_computation.4 | custom fusion | flops 524288 | bytes 6291520 | tf_op jit(solution)/shard_map/transpose(jvp(jit(_take)))/scatter-add | solution.py:53
  65.2 1.6 convolution_convert_fusion.3
  66.8 1.4 convolution_convert_fusion.8
  68.3 1.7 fusion.22
  70.3 4.5 %collective-permute-start.8 = (bf16[1,64,512]{2,1,0:T(8,128)(2,1)S(1)}, bf16[1,64,512]{2,1,0:T(8,128)(2,1)S(1)}, u32[]{:S(2)}, u32[]{:S(2)}) collective-permute-start(bf16[1,64,512]{2,1,0:T(8,128)(2,1)S(1)} %get-tuple-element.43), channel_id=1, source_target_pairs={{0,1},{1,2},{2,3},{3,4},{4,5},{5,6},{6,7},{7,8},{8,9},{9,10},{10,1... | collective-permute-start | bytes 196616 | tf_op jit(solution)/shard_map/ppermute | solution.py:17
  74.9 1.4 collective-permute-start.9
  76.3 2.4 %collective-permute-start.10 = (bf16[1,64,512]{2,1,0:T(8,128)(2,1)S(1)}, bf16[1,64,512]{2,1,0:T(8,128)(2,1)S(1)}, u32[]{:S(2)}, u32[]{:S(2)}) collective-permute-start(bf16[1,64,512]{2,1,0:T(8,128)(2,1)S(1)} %get-tuple-element.45), channel_id=1, source_target_pairs={{0,16},{16,32},{32,48},{48,64},{64,80},{80,96},{96,112},{112,128},... | collective-permute-start | bytes 196616 | tf_op jit(solution)/shard_map/ppermute | solution.py:17
  78.8 2.9 %collective-permute-start.11 = (bf16[1,64,512]{2,1,0:T(8,128)(2,1)S(1)}, bf16[1,64,512]{2,1,0:T(8,128)(2,1)S(1)}, u32[]{:S(2)}, u32[]{:S(2)}) collective-permute-start(bf16[1,64,512]{2,1,0:T(8,128)(2,1)S(1)} %get-tuple-element.44), channel_id=1, source_target_pairs={{16,0},{32,16},{48,32},{64,48},{80,64},{96,80},{112,96},{128,112},... | collective-permute-start | bytes 196616 | tf_op jit(solution)/shard_map/ppermute | solution.py:19
  82.8 0.9 scatter_fusion.1
  83.8 1.6 fusion.29
  85.4 1.4 fusion.4
  86.8 2.7 %fusion.123 = (bf16[4,64,512]{2,1,0:T(8,128)(2,1)S(1)}, f32[4,4,64,512]{3,2,1,0:T(8,128)}) fusion(f32[4,4,64,512]{3,2,1,0:T(8,128)S(1)} %bitcast.148, f32[4,64,512]{2,1,0:T(8,128)S(1)} %copy-done.5, bf16[2,512,512]{2,1,0:T(8,128)(2,1)S(1)} %copy-done.58, bf16[4,64,512]{2,1,0:T(8,128)(2,1)S(1)} %fusion.4), kind=kOutput, calls=%fused_computation.235 | convolution fusion | flops 543031296 | bytes 5767168 | tf_op jit(solution)/shard_map/transpose(jvp())/dot_general | solution.py:55
  89.6 3.5 %scatter_fusion.2 = f32[8,64,512]{2,1,0:T(8,128)S(1)} fusion(f32[8,64,512]{2,1,0:T(8,128)S(1)} %broadcast_in_dim.55, s32[16]{0:T(128)S(1)} %copy-done.49, f32[16,64,512]{2,1,0:T(8,128)} %bitcast.150), kind=kCustom, calls=%fused_computation.6 | custom fusion | flops 524288 | bytes 6291520 | tf_op jit(solution)/shard_map/transpose(jvp(jit(_take)))/scatter-add | solution.py:53
  93.2 1.6 convolution_convert_fusion.2
  94.7 1.4 convolution_convert_fusion.4
  96.1 1.6 fusion.23
  98.1 5.5 %collective-permute-start.12 = (bf16[1,64,512]{2,1,0:T(8,128)(2,1)S(1)}, bf16[1,64,512]{2,1,0:T(8,128)(2,1)S(1)}, u32[]{:S(2)}, u32[]{:S(2)}) collective-permute-start(bf16[1,64,512]{2,1,0:T(8,128)(2,1)S(1)} %get-tuple-element.33), channel_id=1, source_target_pairs={{0,1},{1,2},{2,3},{3,4},{4,5},{5,6},{6,7},{7,8},{8,9},{9,10},{10,1... | collective-permute-start | bytes 196616 | tf_op jit(solution)/shard_map/ppermute | solution.py:17
  103.7 1.3 collective-permute-start.13
  105.0 1.5 collective-permute-start.14
  106.4 3.4 %collective-permute-start.15 = (bf16[1,64,512]{2,1,0:T(8,128)(2,1)S(1)}, bf16[1,64,512]{2,1,0:T(8,128)(2,1)S(1)}, u32[]{:S(2)}, u32[]{:S(2)}) collective-permute-start(bf16[1,64,512]{2,1,0:T(8,128)(2,1)S(1)} %get-tuple-element.34), channel_id=1, source_target_pairs={{16,0},{32,16},{48,32},{64,48},{80,64},{96,80},{112,96},{128,112},... | collective-permute-start | bytes 196616 | tf_op jit(solution)/shard_map/ppermute | solution.py:19
  109.8 87.3 %psum.7 = f32[2,512]{1,0:T(2,128)} all-reduce(f32[2,512]{1,0:T(2,128)S(1)} %pad_maximum_fusion.22), channel_id=1, replica_groups=mesh['lon'=16,'lat'=16] {'lon','lat'}, use_global_device_ids=true, to_apply=%region_20.23 | all-reduce | flops 1024 | bytes 8192 | tf_op jit(solution)/shard_map/psum | solution.py:101
  197.2 0.9 scatter_fusion.3
  (191 shorter events, 15.4 us)
Async XLA Ops:
  0.6 13.9 %copy-start = (f32[1,1,256,512]{3,2,1,0:T(8,128)S(1)}, f32[1,1,256,512]{3,2,1,0:T(8,128)}, u32[]{:S(2)}) copy-start(f32[1,1,256,512]{3,2,1,0:T(8,128)} %param.13) | copy-start | bytes 1572868
  0.6 12.6 %copy-start.53 = (s32[1,1,4,4]{3,2,1,0:T(4,128)S(1)}, s32[1,1,4,4]{3,2,1,0:T(4,128)}, u32[]{:S(2)}) copy-start(s32[1,1,4,4]{3,2,1,0:T(4,128)} %param.16) | copy-start | bytes 196
  0.7 13.3 %copy-start.50 = (f32[2,512]{1,0:T(2,128)S(1)}, f32[2,512]{1,0:T(2,128)}, u32[]{:S(2)}) copy-start(f32[2,512]{1,0:T(2,128)} %param.15) | copy-start | bytes 12292
  0.7 14.1 %copy-start.9 = (bf16[2,1024,512]{2,1,0:T(8,128)(2,1)S(1)}, bf16[2,1024,512]{2,1,0:T(8,128)(2,1)}, u32[]{:S(2)}) copy-start(bf16[2,1024,512]{2,1,0:T(8,128)(2,1)} %param.18) | copy-start | bytes 6291460
  2.2 12.5 %copy-start.52 = (pred[4]{0:T(512)(128)(4,1)}, pred[4]{0:T(512)(128)(4,1)S(1)}, u32[]{:S(2)}) copy-start(pred[4]{0:T(512)(128)(4,1)S(1)} %compare_and_fusion.1) | copy-start | bytes 16
  2.2 12.5 %copy-start.43 = (s32[1024]{0:T(1024)}, s32[1024]{0:T(1024)S(1)}, u32[]{:S(2)}) copy-start(s32[1024]{0:T(1024)S(1)} %pad_clamp_fusion.1) | copy-start | bytes 12292
  3.9 14.0 %copy-start.28 = (bf16[1,64,512]{2,1,0:T(8,128)(2,1)}, bf16[1,64,512]{2,1,0:T(8,128)(2,1)S(1)}, u32[]{:S(2)}) copy-start(bf16[1,64,512]{2,1,0:T(8,128)(2,1)S(1)} %get-tuple-element.61) | copy-start | bytes 196612
  4.0 14.0 %copy-start.29 = (bf16[1,64,512]{2,1,0:T(8,128)(2,1)}, bf16[1,64,512]{2,1,0:T(8,128)(2,1)S(1)}, u32[]{:S(2)}) copy-start(bf16[1,64,512]{2,1,0:T(8,128)(2,1)S(1)} %get-tuple-element.64) | copy-start | bytes 196612
  4.0 15.5 %copy-start.26 = (bf16[1,64,512]{2,1,0:T(8,128)(2,1)}, bf16[1,64,512]{2,1,0:T(8,128)(2,1)S(1)}, u32[]{:S(2)}) copy-start(bf16[1,64,512]{2,1,0:T(8,128)(2,1)S(1)} %get-tuple-element.62) | copy-start | bytes 196612
  4.0 15.5 %copy-start.27 = (bf16[1,64,512]{2,1,0:T(8,128)(2,1)}, bf16[1,64,512]{2,1,0:T(8,128)(2,1)S(1)}, u32[]{:S(2)}) copy-start(bf16[1,64,512]{2,1,0:T(8,128)(2,1)S(1)} %get-tuple-element.63) | copy-start | bytes 196612
  4.0 14.0 %collective-permute-start = (bf16[1,64,512]{2,1,0:T(8,128)(2,1)S(1)}, bf16[1,64,512]{2,1,0:T(8,128)(2,1)S(1)}, u32[]{:S(2)}, u32[]{:S(2)}) collective-permute-start(bf16[1,64,512]{2,1,0:T(8,128)(2,1)S(1)} %get-tuple-element.61), channel_id=1, source_target_pairs={{0,16},{16,32},{32,48},{48,64},{64,80},{80,96},{96,112},{112,128},... | collective-permute-start | bytes 196616 | tf_op jit(solution)/shard_map/ppermute | solution.py:17
  6.7 11.9 %collective-permute-start.1 = (bf16[1,64,512]{2,1,0:T(8,128)(2,1)S(1)}, bf16[1,64,512]{2,1,0:T(8,128)(2,1)}, u32[]{:S(2)}, u32[]{:S(2)}) collective-permute-start(bf16[1,64,512]{2,1,0:T(8,128)(2,1)S(1)} %get-tuple-element.64), channel_id=1, source_target_pairs={{16,0},{32,16},{48,32},{64,48},{80,64},{96,80},{112,96},{128,112},... | collective-permute-start | bytes 196616 | tf_op jit(solution)/shard_map/ppermute | solution.py:19
  7.4 12.1 %collective-permute-start.2 = (bf16[1,64,512]{2,1,0:T(8,128)(2,1)S(1)}, bf16[1,64,512]{2,1,0:T(8,128)(2,1)}, u32[]{:S(2)}, u32[]{:S(2)}) collective-permute-start(bf16[1,64,512]{2,1,0:T(8,128)(2,1)S(1)} %get-tuple-element.63), channel_id=1, source_target_pairs={{0,1},{1,2},{2,3},{3,4},{4,5},{5,6},{6,7},{7,8},{8,9},{9,10},{10,1... | collective-permute-start | bytes 196616 | tf_op jit(solution)/shard_map/ppermute | solution.py:17
  10.8 8.7 %collective-permute-start.3 = (bf16[1,64,512]{2,1,0:T(8,128)(2,1)S(1)}, bf16[1,64,512]{2,1,0:T(8,128)(2,1)}, u32[]{:S(2)}, u32[]{:S(2)}) collective-permute-start(bf16[1,64,512]{2,1,0:T(8,128)(2,1)S(1)} %get-tuple-element.62), channel_id=1, source_target_pairs={{1,0},{2,1},{3,2},{4,3},{5,4},{6,5},{7,6},{8,7},{9,8},{10,9},{11,1... | collective-permute-start | bytes 196616 | tf_op jit(solution)/shard_map/ppermute | solution.py:19
  13.4 7.1 %copy-start.47 = (s32[16]{0:T(128)}, s32[16]{0:T(128)S(1)}, u32[]{:S(2)}) copy-start(s32[16]{0:T(128)S(1)} %compare_select_fusion) | copy-start | bytes 196
  14.0 6.6 %copy-start.31 = (f32[4,64]{1,0:T(4,128)}, f32[4,64]{1,0:T(4,128)S(1)}, u32[]{:S(2)}) copy-start(f32[4,64]{1,0:T(4,128)S(1)} %rsqrt.44) | copy-start | bytes 3076
  15.0 9.6 %copy-start.4 = (f32[4,64,512]{2,1,0:T(8,128)}, f32[4,64,512]{2,1,0:T(8,128)S(1)}, u32[]{:S(2)}) copy-start(f32[4,64,512]{2,1,0:T(8,128)S(1)} %fusion.61) | copy-start | bytes 1572868
  30.0 15.2 %copy-start.41 = (f32[4,64]{1,0:T(4,128)}, f32[4,64]{1,0:T(4,128)S(1)}, u32[]{:S(2)}) copy-start(f32[4,64]{1,0:T(4,128)S(1)} %get-tuple-element.83) | copy-start | bytes 3076
  31.4 14.7 %copy-start.10 = (bf16[2,1024,512]{2,1,0:T(8,128)(2,1)S(1)}, bf16[2,1024,512]{2,1,0:T(8,128)(2,1)}, u32[]{:S(2)}) copy-start(bf16[2,1024,512]{2,1,0:T(8,128)(2,1)} %param.18) | copy-start | bytes 6291460
  32.7 9.0 %collective-permute-start.4 = (bf16[1,64,512]{2,1,0:T(8,128)(2,1)S(1)}, bf16[1,64,512]{2,1,0:T(8,128)(2,1)S(1)}, u32[]{:S(2)}, u32[]{:S(2)}) collective-permute-start(bf16[1,64,512]{2,1,0:T(8,128)(2,1)S(1)} %get-tuple-element.53), channel_id=1, source_target_pairs={{0,16},{16,32},{32,48},{48,64},{64,80},{80,96},{96,112},{112,128},... | collective-permute-start | bytes 196616 | tf_op jit(solution)/shard_map/ppermute | solution.py:17
  34.8 6.9 %collective-permute-start.5 = (bf16[1,64,512]{2,1,0:T(8,128)(2,1)S(1)}, bf16[1,64,512]{2,1,0:T(8,128)(2,1)S(1)}, u32[]{:S(2)}, u32[]{:S(2)}) collective-permute-start(bf16[1,64,512]{2,1,0:T(8,128)(2,1)S(1)} %get-tuple-element.56), channel_id=1, source_target_pairs={{16,0},{32,16},{48,32},{64,48},{80,64},{96,80},{112,96},{128,112},... | collective-permute-start | bytes 196616 | tf_op jit(solution)/shard_map/ppermute | solution.py:19
  35.9 5.9 %collective-permute-start.6 = (bf16[1,64,512]{2,1,0:T(8,128)(2,1)S(1)}, bf16[1,64,512]{2,1,0:T(8,128)(2,1)S(1)}, u32[]{:S(2)}, u32[]{:S(2)}) collective-permute-start(bf16[1,64,512]{2,1,0:T(8,128)(2,1)S(1)} %get-tuple-element.55), channel_id=1, source_target_pairs={{0,1},{1,2},{2,3},{3,4},{4,5},{5,6},{6,7},{7,8},{8,9},{9,10},{10,1... | collective-permute-start | bytes 196616 | tf_op jit(solution)/shard_map/ppermute | solution.py:17
  40.2 5.0 %collective-permute-start.7 = (bf16[1,64,512]{2,1,0:T(8,128)(2,1)S(1)}, bf16[1,64,512]{2,1,0:T(8,128)(2,1)S(1)}, u32[]{:S(2)}, u32[]{:S(2)}) collective-permute-start(bf16[1,64,512]{2,1,0:T(8,128)(2,1)S(1)} %get-tuple-element.54), channel_id=1, source_target_pairs={{1,0},{2,1},{3,2},{4,3},{5,4},{6,5},{7,6},{8,7},{9,8},{10,9},{11,1... | collective-permute-start | bytes 196616 | tf_op jit(solution)/shard_map/ppermute | solution.py:19
  41.7 5.6 %copy-start.35 = (f32[4,64]{1,0:T(4,128)}, f32[4,64]{1,0:T(4,128)S(1)}, u32[]{:S(2)}) copy-start(f32[4,64]{1,0:T(4,128)S(1)} %fusion.109) | copy-start | bytes 3076
  41.7 6.7 %copy-start.14 = (f32[1,64,512]{2,1,0:T(8,128)}, f32[1,64,512]{2,1,0:T(8,128)S(1)}, u32[]{:S(2)}) copy-start(f32[1,64,512]{2,1,0:T(8,128)S(1)} %get-tuple-element.51) | copy-start | bytes 393220
  41.7 6.7 %copy-start.16 = (f32[1,64,512]{2,1,0:T(8,128)}, f32[1,64,512]{2,1,0:T(8,128)S(1)}, u32[]{:S(2)}) copy-start(f32[1,64,512]{2,1,0:T(8,128)S(1)} %get-tuple-element.52) | copy-start | bytes 393220
  45.2 3.2 %copy-start.18 = (f32[1,64,512]{2,1,0:T(8,128)}, f32[1,64,512]{2,1,0:T(8,128)S(1)}, u32[]{:S(2)}) copy-start(f32[1,64,512]{2,1,0:T(8,128)S(1)} %get-tuple-element.57) | copy-start | bytes 393220
  45.2 3.2 %copy-start.20 = (f32[1,64,512]{2,1,0:T(8,128)}, f32[1,64,512]{2,1,0:T(8,128)S(1)}, u32[]{:S(2)}) copy-start(f32[1,64,512]{2,1,0:T(8,128)S(1)} %get-tuple-element.58) | copy-start | bytes 393220
  57.4 4.0 %copy-start.59 = (bf16[4,64,512]{2,1,0:T(8,128)(2,1)}, bf16[4,64,512]{2,1,0:T(8,128)(2,1)S(1)}, u32[]{:S(2)}) copy-start(bf16[4,64,512]{2,1,0:T(8,128)(2,1)S(1)} %fusion.25) | copy-start | bytes 786436
  58.0 3.5 %copy-start.48 = (s32[16]{0:T(128)S(1)}, s32[16]{0:T(128)}, u32[]{:S(2)}) copy-start(s32[16]{0:T(128)} %copy-done.47) | copy-start | bytes 196
  65.1 3.1 %copy-start.15 = (f32[1,64,512]{2,1,0:T(8,128)S(1)}, f32[1,64,512]{2,1,0:T(8,128)}, u32[]{:S(2)}) copy-start(f32[1,64,512]{2,1,0:T(8,128)} %copy-done.14) | copy-start | bytes 393220
  65.1 3.1 %copy-start.17 = (f32[1,64,512]{2,1,0:T(8,128)S(1)}, f32[1,64,512]{2,1,0:T(8,128)}, u32[]{:S(2)}) copy-start(f32[1,64,512]{2,1,0:T(8,128)} %copy-done.16) | copy-start | bytes 393220
  65.1 3.1 %copy-start.19 = (f32[1,64,512]{2,1,0:T(8,128)S(1)}, f32[1,64,512]{2,1,0:T(8,128)}, u32[]{:S(2)}) copy-start(f32[1,64,512]{2,1,0:T(8,128)} %copy-done.18) | copy-start | bytes 393220
  65.2 3.1 %copy-start.21 = (f32[1,64,512]{2,1,0:T(8,128)S(1)}, f32[1,64,512]{2,1,0:T(8,128)}, u32[]{:S(2)}) copy-start(f32[1,64,512]{2,1,0:T(8,128)} %copy-done.20) | copy-start | bytes 393220
  65.2 3.1 %copy-start.36 = (f32[4,64]{1,0:T(4,128)S(1)}, f32[4,64]{1,0:T(4,128)}, u32[]{:S(2)}) copy-start(f32[4,64]{1,0:T(4,128)} %copy-done.35) | copy-start | bytes 3076
  65.2 3.1 %copy-start.38 = (f32[4,64]{1,0:T(4,128)S(1)}, f32[4,64]{1,0:T(4,128)}, u32[]{:S(2)}) copy-start(f32[4,64]{1,0:T(4,128)} %copy-done.37) | copy-start | bytes 3076
  70.3 12.5 %copy-start.45 = (s32[4]{0:T(128)S(1)}, s32[4]{0:T(128)}, u32[]{:S(2)}) copy-start(s32[4]{0:T(128)} %copy-done.44) | copy-start | bytes 52
  70.3 11.9 %collective-permute-start.8 = (bf16[1,64,512]{2,1,0:T(8,128)(2,1)S(1)}, bf16[1,64,512]{2,1,0:T(8,128)(2,1)S(1)}, u32[]{:S(2)}, u32[]{:S(2)}) collective-permute-start(bf16[1,64,512]{2,1,0:T(8,128)(2,1)S(1)} %get-tuple-element.43), channel_id=1, source_target_pairs={{0,1},{1,2},{2,3},{3,4},{4,5},{5,6},{6,7},{7,8},{8,9},{9,10},{10,1... | collective-permute-start | bytes 196616 | tf_op jit(solution)/shard_map/ppermute | solution.py:17
  74.9 8.9 %copy-start.23 = (f32[4,64,512]{2,1,0:T(8,128)S(1)}, f32[4,64,512]{2,1,0:T(8,128)}, u32[]{:S(2)}) copy-start(f32[4,64,512]{2,1,0:T(8,128)} %copy-done.22) | copy-start | bytes 1572868
  74.9 7.4 %collective-permute-start.9 = (bf16[1,64,512]{2,1,0:T(8,128)(2,1)S(1)}, bf16[1,64,512]{2,1,0:T(8,128)(2,1)S(1)}, u32[]{:S(2)}, u32[]{:S(2)}) collective-permute-start(bf16[1,64,512]{2,1,0:T(8,128)(2,1)S(1)} %get-tuple-element.46), channel_id=1, source_target_pairs={{1,0},{2,1},{3,2},{4,3},{5,4},{6,5},{7,6},{8,7},{9,8},{10,9},{11,1... | collective-permute-start | bytes 196616 | tf_op jit(solution)/shard_map/ppermute | solution.py:19
  76.3 5.9 %collective-permute-start.10 = (bf16[1,64,512]{2,1,0:T(8,128)(2,1)S(1)}, bf16[1,64,512]{2,1,0:T(8,128)(2,1)S(1)}, u32[]{:S(2)}, u32[]{:S(2)}) collective-permute-start(bf16[1,64,512]{2,1,0:T(8,128)(2,1)S(1)} %get-tuple-element.45), channel_id=1, source_target_pairs={{0,16},{16,32},{32,48},{48,64},{64,80},{80,96},{96,112},{112,128},... | collective-permute-start | bytes 196616 | tf_op jit(solution)/shard_map/ppermute | solution.py:17
  78.8 4.0 %collective-permute-start.11 = (bf16[1,64,512]{2,1,0:T(8,128)(2,1)S(1)}, bf16[1,64,512]{2,1,0:T(8,128)(2,1)S(1)}, u32[]{:S(2)}, u32[]{:S(2)}) collective-permute-start(bf16[1,64,512]{2,1,0:T(8,128)(2,1)S(1)} %get-tuple-element.44), channel_id=1, source_target_pairs={{16,0},{32,16},{48,32},{64,48},{80,64},{96,80},{112,96},{128,112},... | collective-permute-start | bytes 196616 | tf_op jit(solution)/shard_map/ppermute | solution.py:19
  97.8 12.0 %copy-start.40 = (f32[512]{0:T(512)S(1)}, f32[512]{0:T(512)}, u32[]{:S(2)}) copy-start(f32[512]{0:T(512)} %add.237) | copy-start | bytes 6148
  98.1 99.1 %copy-start.46 = (s32[4]{0:T(128)S(1)}, s32[4]{0:T(128)}, u32[]{:S(2)}) copy-start(s32[4]{0:T(128)} %copy-done.44) | copy-start | bytes 52
  98.1 98.9 %collective-permute-start.12 = (bf16[1,64,512]{2,1,0:T(8,128)(2,1)S(1)}, bf16[1,64,512]{2,1,0:T(8,128)(2,1)S(1)}, u32[]{:S(2)}, u32[]{:S(2)}) collective-permute-start(bf16[1,64,512]{2,1,0:T(8,128)(2,1)S(1)} %get-tuple-element.33), channel_id=1, source_target_pairs={{0,1},{1,2},{2,3},{3,4},{4,5},{5,6},{6,7},{7,8},{8,9},{9,10},{10,1... | collective-permute-start | bytes 196616 | tf_op jit(solution)/shard_map/ppermute | solution.py:17
  103.7 93.4 %collective-permute-start.13 = (bf16[1,64,512]{2,1,0:T(8,128)(2,1)S(1)}, bf16[1,64,512]{2,1,0:T(8,128)(2,1)S(1)}, u32[]{:S(2)}, u32[]{:S(2)}) collective-permute-start(bf16[1,64,512]{2,1,0:T(8,128)(2,1)S(1)} %get-tuple-element.36), channel_id=1, source_target_pairs={{1,0},{2,1},{3,2},{4,3},{5,4},{6,5},{7,6},{8,7},{9,8},{10,9},{11,1... | collective-permute-start | bytes 196616 | tf_op jit(solution)/shard_map/ppermute | solution.py:19
  105.0 92.2 %collective-permute-start.14 = (bf16[1,64,512]{2,1,0:T(8,128)(2,1)S(1)}, bf16[1,64,512]{2,1,0:T(8,128)(2,1)S(1)}, u32[]{:S(2)}, u32[]{:S(2)}) collective-permute-start(bf16[1,64,512]{2,1,0:T(8,128)(2,1)S(1)} %get-tuple-element.35), channel_id=1, source_target_pairs={{0,16},{16,32},{32,48},{48,64},{64,80},{80,96},{96,112},{112,128},... | collective-permute-start | bytes 196616 | tf_op jit(solution)/shard_map/ppermute | solution.py:17
  106.4 90.7 %collective-permute-start.15 = (bf16[1,64,512]{2,1,0:T(8,128)(2,1)S(1)}, bf16[1,64,512]{2,1,0:T(8,128)(2,1)S(1)}, u32[]{:S(2)}, u32[]{:S(2)}) collective-permute-start(bf16[1,64,512]{2,1,0:T(8,128)(2,1)S(1)} %get-tuple-element.34), channel_id=1, source_target_pairs={{16,0},{32,16},{48,32},{64,48},{80,64},{96,80},{112,96},{128,112},... | collective-permute-start | bytes 196616 | tf_op jit(solution)/shard_map/ppermute | solution.py:19
  (30 other events, 59.0 us)
where the time goes:
time: 200 us; the launch traced here: 199 us
  blocking collectives  87.3 us (44%)
  starting transfers between devices  39.9 us (20%)
  matrix products  30.2 us (15%)
  other arithmetic  23 us (12%)
  local copies, waits for them, and re-layouts  12.7 us (6%)
  waiting for transfers between devices  3.94 us (2%)
    psum x1, blocking collectives, local(): grad_gains = lax.psum(jnp.stack(gain_terms), ('lon', 'lat'))  87.3 us
    ppermute x8, starting transfers between devices, padded(): lax.ppermute(tail, axis, [(i, (i + 1) % count) for i in range(ends)])  26.4 us
    ppermute x8, starting transfers between devices, padded(): lax.ppermute(head, axis, [((i + 1) % count, i) for i in range(ends)])  13.6 us
    dot_general x4, matrix products, combine(): messages = jnp.dot(edges, second_edge, preferred_element_type=jnp.float32)  7.51 us
    scatter-add x2, other arithmetic, combine(): jnp.take(project_src, links, axis=0).reshape(nblk, slots, block, width)  7 us
    dot_general x4, matrix products, combine(): jnp.dot(normed, first_node[:width], preferred_element_type=jnp.float32)  6.7 us
    dot_general x4, matrix products, combine(): jnp.dot(sources, first_edge[:width], preferred_element_type=jnp.float32)  6.01 us
    unnamed x124, local copies, waits for them, and re-layouts  5.07 us
  transfers between devices with their start and end apart: 16, of which 2 were waited for; matrix products, arithmetic and copies ran while one was open for 4% of the time, Pallas kernels for 0%

commit v1 on v0

v1 whole, which is shorter than its diff:
```python
import jax
import jax.numpy as jnp
from jax import lax
from jax.experimental import pallas as pl
from jax.experimental.pallas import tpu as pltpu
from jax.sharding import PartitionSpec as P

MESH = pl.DeviceIdType.MESH
F32 = jnp.float32
BF16 = jnp.bfloat16
LAYERS = 2
NBLK = 4
SLOTS = 4
BLOCK = 64
WIDTH = 512
NODES = NBLK * BLOCK
EDGES = NBLK * SLOTS
EPS = 1e-06


def dot(a, b):
    return jnp.dot(a, b, preferred_element_type=F32)


def dot_t(a, b):
    return lax.dot_general(a, b, (((1,), (1,)), ((), ())), preferred_element_type=F32)


def same(a, b):
    apart = a - b
    return 1 - jnp.minimum(apart * apart, 1)


def sigmoid(v):
    return 0.5 * jnp.tanh(0.5 * v) + 0.5


def kernel(
    n_lon, n_lat,
    state, cotangent, gains, senders, picks, edge_in, edge_out, node_in, node_out,
    result, grad_state, grad_gains,
    x, grad, gain, send_ids, pick_ids, w_ei, w_eo, w_ni, w_no,
    xhat, scale, xhat16, normed, outgoing, arrived, normed_far, p_src, p_own,
    slope_edge, slope_node, edge_sum, hidden, total, d_inner, d_total, d_edge,
    chain, d_dst, d_src, back, returned, d_normed,
    gain_mine, gather_lon, gather_lat, gain_out,
    load_sem, weight_sem, out_sem, send_sem, recv_sem, ar_send, ar_recv,
):
    i = lax.axis_index("lon")
    j = lax.axis_index("lat")
    east, west = lax.rem(i + 1, n_lon), lax.rem(i + n_lon - 1, n_lon)
    north, south = lax.rem(j + 1, n_lat), lax.rem(j + n_lat - 1, n_lat)
    ahead = ((east, j), (west, j), (i, north), (i, south))
    behind = ((west, j), (east, j), (i, south), (i, north))
    has_ahead = (None, None, j < n_lat - 1, j > 0)
    has_behind = (None, None, j > 0, j < n_lat - 1)

    barrier = pltpu.get_barrier_semaphore()

    def greet_lon(t, c):
        pl.semaphore_signal(barrier, inc=1, device_id=(lax.rem(i + t, n_lon), j), device_id_type=MESH)
        return c

    def greet_lat(t, c):
        pl.semaphore_signal(barrier, inc=1, device_id=(i, lax.rem(j + t, n_lat)), device_id_type=MESH)
        return c

    lax.fori_loop(1, n_lon, greet_lon, 0)
    lax.fori_loop(1, n_lat, greet_lat, 0)

    loads = [
        pltpu.make_async_copy(state, x.at[0], load_sem.at[0]),
        pltpu.make_async_copy(gains, gain, load_sem.at[1]),
        pltpu.make_async_copy(picks, pick_ids, load_sem.at[2]),
        pltpu.make_async_copy(senders, send_ids, load_sem.at[3]),
        pltpu.make_async_copy(cotangent, grad, load_sem.at[4]),
    ]
    weights = [
        [
            pltpu.make_async_copy(full.at[layer], held.at[layer], weight_sem.at[layer, n])
            for n, (full, held) in enumerate(
                ((edge_in, w_ei), (node_in, w_ni), (edge_out, w_eo), (node_out, w_no))
            )
        ]
        for layer in range(LAYERS)
    ]
    for copy in loads[:4]:
        copy.start()
    for layer in range(LAYERS):
        for copy in weights[layer]:
            copy.start()
    loads[4].start()

    def guarded(when, action):
        if when is None:
            action()
        else:
            pl.when(when)(action)

    def halo(phase, d, src, dst, device):
        return pltpu.make_async_remote_copy(
            src_ref=src, dst_ref=dst,
            send_sem=send_sem.at[phase, d], recv_sem=recv_sem.at[phase, d],
            device_id=device, device_id_type=MESH,
        )

    zero_block = jnp.zeros((BLOCK, WIDTH), BF16)

    def clear(buffer, phase, d):
        buffer[phase, d] = zero_block

    for copy in loads[:4]:
        copy.wait()
    picked = [pick_ids[0, d] for d in range(4)]
    links = [send_ids[e // SLOTS, e % SLOTS] for e in range(EDGES)]

    earlier = []
    for e in range(EDGES):
        found = jnp.int32(EDGES)
        for f in range(e):
            found = found + same(links[f], links[e]) * (f - found)
        earlier.append(found)
    last = []
    for s in range(2 * NBLK):
        found = jnp.int32(EDGES)
        for f in range(EDGES):
            found = found + same(links[f], s) * (f - found)
        last.append(found)

    for layer in range(LAYERS):
        phase = layer
        one_gain = 1.0 + gain[layer : layer + 1, :]

        def norm_rows(c, carry):
            rows = pl.ds(pl.multiple_of(c * 32, 32), 32)
            v = x[layer, rows, :]
            r = lax.rsqrt(jnp.mean(v * v, axis=-1, keepdims=True) + EPS)
            h = v * r
            xhat[layer, rows, :] = h
            scale[layer, rows, :] = jnp.broadcast_to(r, (32, 128))
            xhat16[c // 2, pl.ds(pl.multiple_of((c % 2) * 32, 32), 32), :] = h.astype(BF16)
            normed[rows, :] = (h * one_gain).astype(BF16)
            return carry

        lax.fori_loop(0, NODES // 32, norm_rows, 0)
        for d in range(4):
            outgoing[phase, d] = xhat16[picked[d]]
        if layer == 0:
            pl.semaphore_wait(barrier, n_lon + n_lat - 2)
        sends = [halo(phase, d, outgoing.at[phase, d], arrived.at[phase, d], ahead[d]) for d in range(4)]
        for d in range(4):
            guarded(has_ahead[d], sends[d].start)

        weights[layer][0].wait()
        own = normed[...]
        p_src[0:NBLK] = dot(own, w_ei[layer, 0:WIDTH, :]).reshape(NBLK, BLOCK, WIDTH)
        p_own[:, 0:WIDTH] = dot(own, w_ei[layer, WIDTH : 2 * WIDTH, :])
        weights[layer][1].wait()
        p_own[:, WIDTH : 2 * WIDTH] = dot(own, w_ni[layer, 0:WIDTH, :])

        for d in range(4):
            guarded(has_behind[d], sends[d].wait_recv)
            if has_behind[d] is not None:
                pl.when(jnp.logical_not(has_behind[d]))(lambda d=d: clear(arrived, phase, d))
        for d in range(4):
            normed_far[d * BLOCK : (d + 1) * BLOCK, :] = (arrived[phase, d].astype(F32) * one_gain).astype(BF16)
        p_src[NBLK : 2 * NBLK] = dot(normed_far[...], w_ei[layer, 0:WIDTH, :]).reshape(NBLK, BLOCK, WIDTH)

        def edge_rows(c, carry):
            start = pl.multiple_of(c * 16, 16)
            for b in range(NBLK):
                to = p_own[pl.ds(b * BLOCK + start, 16), 0:WIDTH]
                acc = jnp.zeros((16, WIDTH), F32)
                for k in range(SLOTS):
                    e = b * SLOTS + k
                    pre = p_src[links[e], pl.ds(start, 16), :] + to
                    s = sigmoid(pre)
                    v = pre * s
                    acc = acc + v
                    slope_edge[layer, e, pl.ds(start, 16), :] = (s + v * (1.0 - s)).astype(BF16)
                edge_sum[pl.ds(b * BLOCK + start, 16), :] = acc.astype(BF16)
            return carry

        lax.fori_loop(0, BLOCK // 16, edge_rows, 0)
        weights[layer][2].wait()
        total[...] = dot(edge_sum[...], w_eo[layer]).astype(BF16)
        inner = dot(total[...], w_ni[layer, WIDTH : 2 * WIDTH, :]) + p_own[:, WIDTH : 2 * WIDTH]
        s = sigmoid(inner)
        v = inner * s
        hidden[...] = v.astype(BF16)
        slope_node[layer] = s + v * (1.0 - s)
        weights[layer][3].wait()
        x[layer + 1] = x[layer] + dot(hidden[...], w_no[layer])
        for d in range(4):
            guarded(has_ahead[d], sends[d].wait_send)

    store_result = pltpu.make_async_copy(x.at[LAYERS], result, out_sem.at[0])
    store_result.start()
    loads[4].wait()
    chain[EDGES] = jnp.zeros((BLOCK, WIDTH), F32)

    for layer in reversed(range(LAYERS)):
        phase = 2 * LAYERS - 1 - layer
        back_phase = phase - LAYERS
        one_gain = 1.0 + gain[layer : layer + 1, :]
        d_inner[...] = (dot_t(grad[...].astype(BF16), w_no[layer]) * slope_node[layer]).astype(BF16)
        d_total[...] = dot_t(d_inner[...], w_ni[layer, WIDTH : 2 * WIDTH, :]).astype(BF16)
        d_edge[...] = dot_t(d_total[...], w_eo[layer])

        def slope_rows(c, carry):
            start = pl.multiple_of(c * 16, 16)
            for b in range(NBLK):
                up = d_edge[pl.ds(b * BLOCK + start, 16), :]
                acc = jnp.zeros((16, WIDTH), F32)
                for k in range(SLOTS):
                    e = b * SLOTS + k
                    d_pre = up * slope_edge[layer, e, pl.ds(start, 16), :].astype(F32)
                    acc = acc + d_pre
                    chain[e, pl.ds(start, 16), :] = d_pre + chain[earlier[e], pl.ds(start, 16), :]
                d_dst[pl.ds(b * BLOCK + start, 16), :] = acc.astype(BF16)
            for s in range(2 * NBLK):
                d_src[pl.ds(s * BLOCK + start, 16), :] = chain[last[s], pl.ds(start, 16), :].astype(BF16)
            return carry

        lax.fori_loop(0, BLOCK // 16, slope_rows, 0)
        far = dot_t(d_src[NODES : 2 * NODES, :], w_ei[layer, 0:WIDTH, :]).astype(BF16)
        for d in range(4):
            back[back_phase, d] = far[d * BLOCK : (d + 1) * BLOCK, :]
        sends = [halo(phase, d, back.at[back_phase, d], returned.at[back_phase, d], behind[d]) for d in range(4)]
        for d in range(4):
            guarded(has_behind[d], sends[d].start)

        d_normed[...] = (
            dot_t(d_inner[...], w_ni[layer, 0:WIDTH, :])
            + dot_t(d_dst[...], w_ei[layer, WIDTH : 2 * WIDTH, :])
            + dot_t(d_src[0:NODES, :], w_ei[layer, 0:WIDTH, :])
        )

        def gain_rows(c, acc):
            rows = pl.ds(pl.multiple_of(c * 16, 16), 16)
            near = d_normed[rows, :] * xhat[layer, rows, :]
            part = pl.ds(pl.multiple_of((c % 4) * 16, 16), 16)
            apart = back[back_phase, c // 4, part, :].astype(F32) * arrived[layer, c // 4, part, :].astype(F32)
            return acc + (near + apart)

        acc = lax.fori_loop(0, NODES // 16, gain_rows, jnp.zeros((16, WIDTH), F32))
        acc = jnp.sum(acc, axis=0, keepdims=True)
        for q in range(4):
            gain_mine[layer * 4 + q : layer * 4 + q + 1, :] = acc[:, q * 128 : (q + 1) * 128]

        if layer == 0:

            def lon_copy(t):
                return pltpu.make_async_remote_copy(
                    src_ref=gain_mine, dst_ref=gather_lon.at[i],
                    send_sem=ar_send.at[0, t], recv_sem=ar_recv.at[0, t],
                    device_id=(lax.rem(i + t, n_lon), j), device_id_type=MESH,
                )

            def lon_start(t, c):
                lon_copy(t).start()
                return c

            lax.fori_loop(1, n_lon, lon_start, 0)
            gather_lon[i] = gain_mine[...]

        for d in range(4):
            guarded(has_ahead[d], sends[d].wait_recv)
            if has_ahead[d] is not None:
                pl.when(jnp.logical_not(has_ahead[d]))(lambda d=d: clear(returned, back_phase, d))

        chosen = [[same(picked[d], b).astype(F32) for d in range(4)] for b in range(NBLK)]

        def norm_back(c, carry):
            start = pl.multiple_of(c * 16, 16)
            sent = [returned[back_phase, d, pl.ds(start, 16), :].astype(F32) for d in range(4)]
            for b in range(NBLK):
                rows = pl.ds(b * BLOCK + start, 16)
                dn = d_normed[rows, :]
                for d in range(4):
                    dn = dn + chosen[b][d] * sent[d]
                dh = dn * one_gain
                h = xhat[layer, rows, :]
                along = jnp.mean(dh * h, axis=-1, keepdims=True)
                r = scale[layer, rows, 0:1]
                grad[rows, :] = grad[rows, :] + r * (dh - h * along)
            return carry

        lax.fori_loop(0, BLOCK // 16, norm_back, 0)
        for d in range(4):
            guarded(has_behind[d], sends[d].wait_send)

    store_grad = pltpu.make_async_copy(grad, grad_state, out_sem.at[1])
    store_grad.start()

    def lon_wait(t, c):
        pltpu.make_async_remote_copy(
            src_ref=gain_mine, dst_ref=gather_lon.at[lax.rem(i + n_lon - t, n_lon)],
            send_sem=ar_send.at[0, t], recv_sem=ar_recv.at[0, t],
            device_id=(lax.rem(i + t, n_lon), j), device_id_type=MESH,
        ).wait()
        return c

    lax.fori_loop(1, n_lon, lon_wait, 0)
    partial_sum = gather_lon[0]
    for t in range(1, n_lon):
        partial_sum = partial_sum + gather_lon[t]
    gain_mine[...] = partial_sum

    def lat_copy(t, slot):
        return pltpu.make_async_remote_copy(
            src_ref=gain_mine, dst_ref=gather_lat.at[slot],
            send_sem=ar_send.at[1, t], recv_sem=ar_recv.at[1, t],
            device_id=(i, lax.rem(j + t, n_lat)), device_id_type=MESH,
        )

    def lat_start(t, c):
        lat_copy(t, j).start()
        return c

    def lat_wait(t, c):
        lat_copy(t, lax.rem(j + n_lat - t, n_lat)).wait()
        return c

    lax.fori_loop(1, n_lat, lat_start, 0)
    gather_lat[j] = partial_sum
    lax.fori_loop(1, n_lat, lat_wait, 0)
    whole = gather_lat[0]
    for t in range(1, n_lat):
        whole = whole + gather_lat[t]
    for layer in range(LAYERS):
        for q in range(4):
            gain_out[layer : layer + 1, q * 128 : (q + 1) * 128] = whole[layer * 4 + q : layer * 4 + q + 1, :]
    store_gain = pltpu.make_async_copy(gain_out, grad_gains, out_sem.at[2])
    store_gain.start()
    store_gain.wait()
    store_grad.wait()
    store_result.wait()


def solution(mesh):
    n_lon, n_lat = mesh.shape["lon"], mesh.shape["lat"]

    def local(state, cotangent, gains, senders, halo_map, edge_in, edge_out, node_in, node_out):
        anywhere = pl.BlockSpec(memory_space=pl.ANY)
        vmem = pltpu.VMEM
        shape = (1, 1, NODES, WIDTH)
        rows = (NODES, WIDTH)
        scratch = [
            vmem((LAYERS + 1,) + rows, F32),
            vmem(rows, F32),
            vmem((LAYERS, WIDTH), F32),
            pltpu.SMEM((NBLK, SLOTS), jnp.int32),
            pltpu.SMEM((1, 4), jnp.int32),
            vmem((LAYERS, 2 * WIDTH, WIDTH), BF16),
            vmem((LAYERS, WIDTH, WIDTH), BF16),
            vmem((LAYERS, 2 * WIDTH, WIDTH), BF16),
            vmem((LAYERS, WIDTH, WIDTH), BF16),
            vmem((LAYERS,) + rows, F32),
            vmem((LAYERS, NODES, 128), F32),
            vmem((NBLK, BLOCK, WIDTH), BF16),
            vmem(rows, BF16),
            vmem((LAYERS, 4, BLOCK, WIDTH), BF16),
            vmem((LAYERS, 4, BLOCK, WIDTH), BF16),
            vmem(rows, BF16),
            vmem((2 * NBLK, BLOCK, WIDTH), F32),
            vmem((NODES, 2 * WIDTH), F32),
            vmem((LAYERS, EDGES, BLOCK, WIDTH), BF16),
            vmem((LAYERS,) + rows, F32),
            vmem(rows, BF16),
            vmem(rows, BF16),
            vmem(rows, BF16),
            vmem(rows, BF16),
            vmem(rows, BF16),
            vmem(rows, F32),
            vmem((EDGES + 1, BLOCK, WIDTH), F32),
            vmem(rows, BF16),
            vmem((2 * NODES, WIDTH), BF16),
            vmem((LAYERS, 4, BLOCK, WIDTH), BF16),
            vmem((LAYERS, 4, BLOCK, WIDTH), BF16),
            vmem(rows, F32),
            vmem((8, 128), F32),
            vmem((n_lon, 8, 128), F32),
            vmem((n_lat, 8, 128), F32),
            vmem((LAYERS, WIDTH), F32),
            pltpu.SemaphoreType.DMA((5,)),
            pltpu.SemaphoreType.DMA((LAYERS, 4)),
            pltpu.SemaphoreType.DMA((3,)),
            pltpu.SemaphoreType.DMA((2 * LAYERS, 4)),
            pltpu.SemaphoreType.DMA((2 * LAYERS, 4)),
            pltpu.SemaphoreType.DMA((2, max(n_lon, n_lat))),
            pltpu.SemaphoreType.DMA((2, max(n_lon, n_lat))),
        ]
        result, grad_state, grad_gains = pl.pallas_call(
            lambda *refs: kernel(n_lon, n_lat, *refs),
            out_shape=(
                jax.ShapeDtypeStruct(rows, F32),
                jax.ShapeDtypeStruct(rows, F32),
                jax.ShapeDtypeStruct((LAYERS, WIDTH), F32),
            ),
            in_specs=[anywhere] * 9,
            out_specs=(anywhere,) * 3,
            scratch_shapes=scratch,
            compiler_params=pltpu.CompilerParams(
                collective_id=0, has_side_effects=True, vmem_limit_bytes=48 * 2**20
            ),
            cost_estimate=pl.CostEstimate(flops=4 * 10**9, bytes_accessed=10**7, transcendentals=2 * 10**6),
            name="mesh_steps",
        )(
            state.reshape(rows),
            cotangent.reshape(rows),
            gains,
            senders.reshape(NBLK, SLOTS),
            halo_map.reshape(1, 4),
            edge_in,
            edge_out,
            node_in,
            node_out,
        )
        return result.reshape(shape), grad_state.reshape(shape), grad_gains

    split = P("lon", "lat", None, None)
    return jax.shard_map(
        local,
        mesh=mesh,
        in_specs=(split, split, P(), split, split, P(), P(), P(), P()),
        out_specs=(split, split, P()),
        check_vma=False,
    )
```

time: 200 us -> 54.3 us (0.27)
  blocking collectives: 87.3 us -> 0 us
  Pallas kernels: 0 us -> 44.6 us
  starting transfers between devices: 39.9 us -> 0 us
  matrix products: 30.2 us -> 0 us
  other arithmetic: 23 us -> 0 us
  local copies, waits for them, and re-layouts: 12.7 us -> 8.73 us
  waiting for transfers between devices: 3.94 us -> 0 us
    psum x1 -> x0, blocking collectives: 87.3 us -> none  [local(): grad_gains = lax.psum(jnp.stack(gain_terms), ('lon', 'lat'))]
    pallas_call x0 -> x1, Pallas kernels: none -> 44.6 us  [local(): pl.pallas_call(lambda *refs: kernel(n_lon, n_lat, *refs), out_shape=(jax....]
    ppermute x16 -> x0, starting transfers between devices: 39.9 us -> none  [the longest x8 26.4 us: padded(): lax.ppermute(tail, axis, [(i, (i + 1) % count) for i in range(ends)])]
    dot_general x24 -> x0, matrix products: 30.2 us -> none  [the longest x4 7.51 us: combine(): messages = jnp.dot(edges, second_edge, preferred_element_type=jnp.float32)]
    scatter-add x4 -> x0, other arithmetic: 8.75 us -> none  [the longest x2 7 us: combine(): jnp.take(project_src, links, axis=0).reshape(nblk, slots, block, width)]
    gather x4 -> x0, local copies, waits for them, and re-layouts: 7.07 us -> none  [the longest x2 4.05 us: combine(): jnp.take(project_src, links, axis=0).reshape(nblk, slots, block, width)]
    convert_element_type x5 -> x0, other arithmetic: 5.15 us -> none  [the longest x2 4.08 us: combine(): edges = jax.nn.silu(chosen + project_dst[:, None]).astype(jnp.bfloat16)]
    ppermute x16 -> x0, waiting for transfers between devices: 3.94 us -> none  [the longest x8 3.92 us: padded(): lax.ppermute(head, axis, [((i + 1) % count, i) for i in range(ends)])]
  transfers between devices with their start and end apart: 16 -> 0, of which waited for: 2 -> 0; matrix products, arithmetic and copies ran while one was open for 4% -> 0% of each run, Pallas kernels for 0% -> 0%
where the time goes in v1:
time: 54.3 us; the launch traced here: 53.9 us
  Pallas kernels  44.6 us (82%)
  local copies, waits for them, and re-layouts  8.73 us (16%)
  between operations  0.66 us (1%)
    pallas_call x1, Pallas kernels, local(): pl.pallas_call(lambda *refs: kernel(n_lon, n_lat, *refs), out_shape=(jax....  44.6 us
    unnamed x17, local copies, waits for them, and re-layouts  8.73 us

profile of v1, /device:TPU:1, one launch (start us, length us, event | category | flops | bytes accessed | tf_op | source)
XLA Modules:
  0.0 53.9 jit_solution(9678709232011827182)
XLA Ops:
  0.6 0.0 copy-start
  0.6 1.2 %copy-done = bf16[2,512,512]{2,1,0:T(8,128)(2,1)S(1)} copy-done((bf16[2,512,512]{2,1,0:T(8,128)(2,1)S(1)}, bf16[2,512,512]{2,1,0:T(8,128)(2,1)}, u32[]{:S(2)}) %copy-start) | copy-done | bytes 1048600
  1.9 0.0 copy-start.1
  1.9 1.2 %copy-done.1 = bf16[2,512,512]{2,1,0:T(8,128)(2,1)S(1)} copy-done((bf16[2,512,512]{2,1,0:T(8,128)(2,1)S(1)}, bf16[2,512,512]{2,1,0:T(8,128)(2,1)}, u32[]{:S(2)}) %copy-start.1) | copy-done | bytes 1048600
  3.1 0.0 copy-start.2
  3.1 1.0 %copy-done.2 = f32[1,1,256,512]{3,2,1,0:T(8,128)S(1)} copy-done((f32[1,1,256,512]{3,2,1,0:T(8,128)S(1)}, f32[1,1,256,512]{3,2,1,0:T(8,128)}, u32[]{:S(2)}) %copy-start.2) | copy-done | bytes 524312
  4.1 0.0 copy-start.3
  4.1 1.0 %copy-done.3 = f32[1,1,256,512]{3,2,1,0:T(8,128)S(1)} copy-done((f32[1,1,256,512]{3,2,1,0:T(8,128)S(1)}, f32[1,1,256,512]{3,2,1,0:T(8,128)}, u32[]{:S(2)}) %copy-start.3) | copy-done | bytes 524312
  5.2 0.0 copy-start.4
  5.2 0.7 %copy-done.4 = f32[2,512]{1,0:T(2,128)S(1)} copy-done((f32[2,512]{1,0:T(2,128)S(1)}, f32[2,512]{1,0:T(2,128)}, u32[]{:S(2)}) %copy-start.4) | copy-done | bytes 4120
  5.9 0.0 copy-start.5
  5.9 0.7 %copy-done.5 = s32[1,1,4,4]{3,2,1,0:T(4,128)S(1)} copy-done((s32[1,1,4,4]{3,2,1,0:T(4,128)S(1)}, s32[1,1,4,4]{3,2,1,0:T(4,128)}, u32[]{:S(2)}) %copy-start.5) | copy-done | bytes 88
  6.5 0.0 copy-start.6
  6.5 0.7 %copy-done.6 = s32[1,1,4,1]{2,3,1,0:T(1,128)S(1)} copy-done((s32[1,1,4,1]{2,3,1,0:T(1,128)S(1)}, s32[1,1,4,1]{2,3,1,0:T(1,128)}, u32[]{:S(2)}) %copy-start.6) | copy-done | bytes 40
  7.2 44.6 %mesh_steps.1 = (f32[256,512]{1,0:T(8,128)S(1)}, f32[256,512]{1,0:T(8,128)S(1)}, f32[2,512]{1,0:T(2,128)S(1)}) custom-call(f32[256,512]{1,0:T(8,128)S(1)} %bitcast.8, f32[256,512]{1,0:T(8,128)S(1)} %bitcast.9, f32[2,512]{1,0:T(2,128)S(1)} %copy-done.4, s32[4,4]{1,0:T(4,128)S(1)} %bitcast.10, s32[1,4]{1,0:T(1,128)S(1)} %bitcast.11, ...), custom_call_target="tpu_custom_call" | custom-call | flops 4000000000 | bytes 10000000 | tf_op jit(solution)/shard_map/mesh_steps/pallas_call | solution.py:394
  51.8 0.8 %copy.15 = f32[1,1,256,512]{3,2,1,0:T(8,128)} copy(f32[1,1,256,512]{3,2,1,0:T(8,128)S(1)} %bitcast.7) | data formatting | bytes 1048576
  52.5 0.8 %copy.16 = f32[1,1,256,512]{3,2,1,0:T(8,128)} copy(f32[1,1,256,512]{3,2,1,0:T(8,128)S(1)} %bitcast.6) | data formatting | bytes 1048576
  53.3 0.6 %copy.17 = f32[2,512]{1,0:T(2,128)} copy(f32[2,512]{1,0:T(2,128)S(1)} %get-tuple-element.14) | data formatting | bytes 8192
Async XLA Ops:
  0.6 1.2 %copy-start = (bf16[2,512,512]{2,1,0:T(8,128)(2,1)S(1)}, bf16[2,512,512]{2,1,0:T(8,128)(2,1)}, u32[]{:S(2)}) copy-start(bf16[2,512,512]{2,1,0:T(8,128)(2,1)} %refs_6_.1) | copy-start | bytes 3145732
  1.9 1.2 %copy-start.1 = (bf16[2,512,512]{2,1,0:T(8,128)(2,1)S(1)}, bf16[2,512,512]{2,1,0:T(8,128)(2,1)}, u32[]{:S(2)}) copy-start(bf16[2,512,512]{2,1,0:T(8,128)(2,1)} %refs_8_.1) | copy-start | bytes 3145732
  3.1 1.0 %copy-start.2 = (f32[1,1,256,512]{3,2,1,0:T(8,128)S(1)}, f32[1,1,256,512]{3,2,1,0:T(8,128)}, u32[]{:S(2)}) copy-start(f32[1,1,256,512]{3,2,1,0:T(8,128)} %param.9) | copy-start | bytes 1572868
  4.1 1.0 %copy-start.3 = (f32[1,1,256,512]{3,2,1,0:T(8,128)S(1)}, f32[1,1,256,512]{3,2,1,0:T(8,128)}, u32[]{:S(2)}) copy-start(f32[1,1,256,512]{3,2,1,0:T(8,128)} %param.10) | copy-start | bytes 1572868
  5.2 0.7 %copy-start.4 = (f32[2,512]{1,0:T(2,128)S(1)}, f32[2,512]{1,0:T(2,128)}, u32[]{:S(2)}) copy-start(f32[2,512]{1,0:T(2,128)} %refs_2_.1) | copy-start | bytes 12292
  5.9 0.7 %copy-start.5 = (s32[1,1,4,4]{3,2,1,0:T(4,128)S(1)}, s32[1,1,4,4]{3,2,1,0:T(4,128)}, u32[]{:S(2)}) copy-start(s32[1,1,4,4]{3,2,1,0:T(4,128)} %param.12) | copy-start | bytes 196
  6.5 0.7 %copy-start.6 = (s32[1,1,4,1]{2,3,1,0:T(1,128)S(1)}, s32[1,1,4,1]{2,3,1,0:T(1,128)}, u32[]{:S(2)}) copy-start(s32[1,1,4,1]{2,3,1,0:T(1,128)} %param.13) | copy-start | bytes 52

commit v2 on v1

--- a/solution.py
+++ b/solution.py
@@ -54,19 +54,6 @@
     behind = ((west, j), (east, j), (i, south), (i, north))
     has_ahead = (None, None, j < n_lat - 1, j > 0)
     has_behind = (None, None, j > 0, j < n_lat - 1)
-
-    barrier = pltpu.get_barrier_semaphore()
-
-    def greet_lon(t, c):
-        pl.semaphore_signal(barrier, inc=1, device_id=(lax.rem(i + t, n_lon), j), device_id_type=MESH)
-        return c
-
-    def greet_lat(t, c):
-        pl.semaphore_signal(barrier, inc=1, device_id=(i, lax.rem(j + t, n_lat)), device_id_type=MESH)
-        return c
-
-    lax.fori_loop(1, n_lon, greet_lon, 0)
-    lax.fori_loop(1, n_lat, greet_lat, 0)
 
     loads = [
         pltpu.make_async_copy(state, x.at[0], load_sem.at[0]),
@@ -91,6 +78,19 @@
             copy.start()
     loads[4].start()
 
+    barrier = pltpu.get_barrier_semaphore()
+
+    def greet_lon(t, c):
+        pl.semaphore_signal(barrier, inc=1, device_id=(lax.rem(i + t, n_lon), j), device_id_type=MESH)
+        return c
+
+    def greet_lat(t, c):
+        pl.semaphore_signal(barrier, inc=1, device_id=(i, lax.rem(j + t, n_lat)), device_id_type=MESH)
+        return c
+
+    lax.fori_loop(1, n_lon, greet_lon, 0)
+    lax.fori_loop(1, n_lat, greet_lat, 0)
+
     def guarded(when, action):
         if when is None:
             action()
@@ -142,7 +142,7 @@
             normed[rows, :] = (h * one_gain).astype(BF16)
             return carry
 
-        lax.fori_loop(0, NODES // 32, norm_rows, 0)
+        lax.fori_loop(0, NODES // 32, norm_rows, 0, unroll=True)
         for d in range(4):
             outgoing[phase, d] = xhat16[picked[d]]
         if layer == 0:
@@ -181,7 +181,7 @@
                 edge_sum[pl.ds(b * BLOCK + start, 16), :] = acc.astype(BF16)
             return carry
 
-        lax.fori_loop(0, BLOCK // 16, edge_rows, 0)
+        lax.fori_loop(0, BLOCK // 16, edge_rows, 0, unroll=2)
         weights[layer][2].wait()
         total[...] = dot(edge_sum[...], w_eo[layer]).astype(BF16)
         inner = dot(total[...], w_ni[layer, WIDTH : 2 * WIDTH, :]) + p_own[:, WIDTH : 2 * WIDTH]
@@ -222,7 +222,7 @@
                 d_src[pl.ds(s * BLOCK + start, 16), :] = chain[last[s], pl.ds(start, 16), :].astype(BF16)
             return carry
 
-        lax.fori_loop(0, BLOCK // 16, slope_rows, 0)
+        lax.fori_loop(0, BLOCK // 16, slope_rows, 0, unroll=2)
         far = dot_t(d_src[NODES : 2 * NODES, :], w_ei[layer, 0:WIDTH, :]).astype(BF16)
         for d in range(4):
             back[back_phase, d] = far[d * BLOCK : (d + 1) * BLOCK, :]
@@ -286,7 +286,7 @@
                 grad[rows, :] = grad[rows, :] + r * (dh - h * along)
             return carry
 
-        lax.fori_loop(0, BLOCK // 16, norm_back, 0)
+        lax.fori_loop(0, BLOCK // 16, norm_back, 0, unroll=True)
         for d in range(4):
             guarded(has_behind[d], sends[d].wait_send)
 
@@ -342,7 +342,7 @@
     n_lon, n_lat = mesh.shape["lon"], mesh.shape["lat"]
 
     def local(state, cotangent, gains, senders, halo_map, edge_in, edge_out, node_in, node_out):
-        anywhere = pl.BlockSpec(memory_space=pl.ANY)
+        anywhere = pl.BlockSpec(memory_space=pltpu.HBM)
         vmem = pltpu.VMEM
         shape = (1, 1, NODES, WIDTH)
         rows = (NODES, WIDTH)
@@ -402,7 +402,7 @@
             out_specs=(anywhere,) * 3,
             scratch_shapes=scratch,
             compiler_params=pltpu.CompilerParams(
-                collective_id=0, has_side_effects=True, vmem_limit_bytes=48 * 2**20
+                collective_id=0, has_side_effects=True, vmem_limit_bytes=60 * 2**20
             ),
             cost_estimate=pl.CostEstimate(flops=4 * 10**9, bytes_accessed=10**7, transcendentals=2 * 10**6),
             name="mesh_steps",

time: 54.3 us -> 49.6 us (0.913)
  local copies, waits for them, and re-layouts: 8.73 us -> 4.33 us
    unnamed x17 -> x5, local copies, waits for them, and re-layouts: 8.73 us -> 4.33 us
where the time goes in v2:
time: 49.6 us; the launch traced here: 49.5 us
  Pallas kernels  44.5 us (90%)
  local copies, waits for them, and re-layouts  4.33 us (9%)
  between operations  0.65 us (1%)
    pallas_call x1, Pallas kernels, local(): pl.pallas_call(lambda *refs: kernel(n_lon, n_lat, *refs), out_shape=(jax....  44.5 us
    unnamed x5, local copies, waits for them, and re-layouts  4.33 us

profile of v2, /device:TPU:1, one launch (start us, length us, event | category | flops | bytes accessed | tf_op | source)
XLA Modules:
  0.0 49.5 jit_solution(10630360710200112004)
XLA Ops:
  0.6 44.5 %mesh_steps.1 = (f32[256,512]{1,0:T(8,128)}, f32[256,512]{1,0:T(8,128)}, f32[2,512]{1,0:T(2,128)}) custom-call(f32[256,512]{1,0:T(8,128)} %bitcast.8, f32[256,512]{1,0:T(8,128)} %bitcast.9, f32[2,512]{1,0:T(2,128)} %refs_2_.1, s32[4,4]{1,0:T(4,128)} %bitcast.10, s32[1,4]{1,0:T(1,128)} %bitcast.11, bf16[2,1024,512]{2,1,0:T(8,128)(2,1)} %refs_5_.1, ...), custom_call_target="tpu_custom_call" | custom-call | flops 4000000000 | bytes 10000000 | tf_op jit(solution)/shard_map/mesh_steps/pallas_call | solution.py:394
  45.1 0.0 copy-start
  45.1 1.9 %copy.15 = f32[1,1,256,512]{3,2,1,0:T(8,128)} copy(f32[1,1,256,512]{3,2,1,0:T(8,128)} %bitcast.7) | data formatting | bytes 1048576
  47.0 1.9 %copy.16 = f32[1,1,256,512]{3,2,1,0:T(8,128)} copy(f32[1,1,256,512]{3,2,1,0:T(8,128)} %bitcast.6) | data formatting | bytes 1048576
  48.9 0.0 copy-done
  48.9 0.6 %copy.17 = f32[2,512]{1,0:T(2,128)} copy(f32[2,512]{1,0:T(2,128)S(1)} %copy-done) | data formatting | bytes 8192
Async XLA Ops:
  45.1 3.7 %copy-start = (f32[2,512]{1,0:T(2,128)S(1)}, f32[2,512]{1,0:T(2,128)}, u32[]{:S(2)}) copy-start(f32[2,512]{1,0:T(2,128)} %get-tuple-element.14) | copy-start | bytes 12292

commit v3 on v0

v3 whole, which is shorter than its diff:
```python
import jax
import jax.numpy as jnp
from jax import lax
from jax.experimental import pallas as pl
from jax.experimental.pallas import tpu as pltpu
from jax.sharding import PartitionSpec as P

MESH = pl.DeviceIdType.MESH
F32 = jnp.float32
BF16 = jnp.bfloat16
LAYERS = 2
NBLK = 4
SLOTS = 4
BLOCK = 64
WIDTH = 512
EDGES = NBLK * SLOTS
STREAMS = 2
PART = BLOCK // STREAMS
ROWS = NBLK * PART
CHUNK = 16
EPS = 1e-06


def dot(a, b):
    return jnp.dot(a, b, preferred_element_type=F32)


def same(a, b):
    apart = a - b
    return 1 - jnp.minimum(apart * apart, 1)


def sigmoid(v):
    return 0.5 * jnp.tanh(0.5 * v) + 0.5


def chunks():
    return [pl.ds(c * CHUNK, CHUNK) for c in range(PART // CHUNK)]


def kernel(
    n_lon, n_lat,
    state, cotangent, gains, senders, picks, edge_in, edge_out, node_in, node_out,
    result, grad, grad_gains,
    x, gain, send_ids, pick_ids, w_ei, w_eo, w_ni, w_no, flip_no, flip_total, flip_eo, flip_in,
    xhat, scale, xhat16, normed, outgoing, arrived, normed_far, p_src, p_own,
    slope_edge, slope_node, edge_sum, hidden, total, d_total, d_edge,
    chain, d_own, d_far, back, returned, d_normed,
    gain_mine, gain_near, gather_near, gather_far,
    load_sem, weight_sem, send_sem, recv_sem, ar_send, ar_recv,
):
    i = lax.axis_index("lon")
    j = lax.axis_index("lat")
    east, west = lax.rem(i + 1, n_lon), lax.rem(i + n_lon - 1, n_lon)
    north, south = lax.rem(j + 1, n_lat), lax.rem(j + n_lat - 1, n_lat)
    ahead = ((east, j), (west, j), (i, north), (i, south))
    behind = ((west, j), (east, j), (i, south), (i, north))
    has_ahead = (None, None, j < n_lat - 1, j > 0)
    has_behind = (None, None, j > 0, j < n_lat - 1)

    small = [
        pltpu.make_async_copy(picks, pick_ids, load_sem.at[0]),
        pltpu.make_async_copy(senders, send_ids, load_sem.at[1]),
        pltpu.make_async_copy(gains, gain, load_sem.at[2]),
    ]
    load_x = [
        pltpu.make_async_copy(state.at[:, pl.ds(h * PART, PART), :], x.at[0, h], load_sem.at[3 + h])
        for h in range(STREAMS)
    ]
    load_g = pltpu.make_async_copy(cotangent, grad, load_sem.at[3 + STREAMS])
    weights = [
        [
            pltpu.make_async_copy(full.at[layer], held.at[layer], weight_sem.at[layer, n])
            for n, (full, held) in enumerate(
                ((edge_in, w_ei), (node_in, w_ni), (edge_out, w_eo), (node_out, w_no))
            )
        ]
        for layer in range(LAYERS)
    ]
    for copy in small + load_x:
        copy.start()

    barrier = pltpu.get_barrier_semaphore()

    depth, columns = n_lat // 2, n_lon // 2
    core, column, high, z = i % 2, i // 2, j // depth, j % depth
    near_slot, far_slot = core * depth + z, column * 2 + high
    apart = lambda t, n: min(t, n - t)
    near = [
        (column * 2 + (core + c) % 2, high * depth + (z + t) % depth)
        for t in sorted(range(depth), key=lambda t: -apart(t, depth)) for c in range(2) if c + t > 0
    ]
    far = [
        ((column + t) % columns * 2 + core, (high + c) % 2 * depth + z)
        for c in (1, 0) for t in sorted(range(columns), key=lambda t: -apart(t, columns)) if c + t > 0
    ]
    for device in ahead + tuple(near) + tuple(far):
        pl.semaphore_signal(barrier, inc=1, device_id=device, device_id_type=MESH)
    for layer in range(LAYERS):
        for copy in weights[layer]:
            copy.start()
    load_g.start()

    def guarded(when, action):
        if when is None:
            action()
        else:
            pl.when(when)(action)

    zeros = jnp.zeros((PART, WIDTH), BF16)
    for d in (2, 3):

        def clear_arrived(d=d):
            for layer in range(LAYERS):
                for h in range(STREAMS):
                    arrived[layer, h, d] = zeros

        def clear_returned(d=d):
            for layer in range(LAYERS):
                for h in range(STREAMS):
                    returned[layer, h, d] = zeros

        pl.when(jnp.logical_not(has_behind[d]))(clear_arrived)
        pl.when(jnp.logical_not(has_ahead[d]))(clear_returned)
    chain[EDGES] = jnp.zeros((PART, WIDTH), F32)

    for copy in small:
        copy.wait()
    picked = [pick_ids[0, d] for d in range(4)]
    links = [send_ids[e // SLOTS, e % SLOTS] for e in range(EDGES)]
    chosen = [[same(picked[d], b).astype(F32) for d in range(4)] for b in range(NBLK)]

    earlier = []
    for e in range(EDGES):
        found = jnp.int32(EDGES)
        for f in range(e):
            found = found + same(links[f], links[e]) * (f - found)
        earlier.append(found)
    last = []
    for s in range(2 * NBLK):
        found = jnp.int32(EDGES)
        for f in range(EDGES):
            found = found + same(links[f], s) * (f - found)
        last.append(found)

    one_gain = [None] * LAYERS

    def halo(phase, h, d):
        if phase < LAYERS:
            src, dst, device = outgoing.at[phase, h, d], arrived.at[phase, h, d], ahead[d]
        else:
            layer = 2 * LAYERS - 1 - phase
            src, dst, device = back.at[layer, h, d], returned.at[layer, h, d], behind[d]
        return pltpu.make_async_remote_copy(
            src_ref=src, dst_ref=dst,
            send_sem=send_sem.at[phase, h, d], recv_sem=recv_sem.at[phase, h, d],
            device_id=device, device_id_type=MESH,
        )

    order = (2, 3, 0, 1)

    def start_halo(phase, h):
        for d in order:
            guarded((has_ahead if phase < LAYERS else has_behind)[d], halo(phase, h, d).start)

    def wait_halo(phase, h):
        for d in order:
            guarded((has_behind if phase < LAYERS else has_ahead)[d], halo(phase, h, d).wait_recv)

    def norm(layer, h):
        for b in range(NBLK):
            v = x[layer, h, b]
            r = lax.rsqrt(jnp.mean(v * v, axis=-1, keepdims=True) + EPS)
            unit = v * r
            xhat[layer, h, b] = unit
            scale[layer, h, b] = jnp.broadcast_to(r, (PART, 128))
            xhat16[h, b] = unit.astype(BF16)
            normed[h, b * PART : (b + 1) * PART, :] = (unit * one_gain[layer]).astype(BF16)

    def send(layer, h):
        for d in range(4):
            outgoing[layer, h, d] = xhat16[h, picked[d]]
        start_halo(layer, h)

    def own(layer, h):
        if layer == 0 and h == 0:
            weights[layer][0].wait()
            weights[layer][1].wait()
        rows = normed[h]
        p_src[h, 0:NBLK] = dot(rows, w_ei[layer, 0:WIDTH, :]).reshape(NBLK, PART, WIDTH)
        p_own[h, :, 0:WIDTH] = dot(rows, w_ei[layer, WIDTH : 2 * WIDTH, :])
        p_own[h, :, WIDTH : 2 * WIDTH] = dot(rows, w_ni[layer, 0:WIDTH, :])

    def finish(layer, h):
        wait_halo(layer, h)
        for d in range(4):
            normed_far[h, d * PART : (d + 1) * PART, :] = (
                arrived[layer, h, d].astype(F32) * one_gain[layer]
            ).astype(BF16)
        p_src[h, NBLK : 2 * NBLK] = dot(normed_far[h], w_ei[layer, 0:WIDTH, :]).reshape(NBLK, PART, WIDTH)
        for c, rows in enumerate(chunks()):
            for b in range(NBLK):
                at = pl.ds(b * PART + c * CHUNK, CHUNK)
                to = p_own[h, at, 0:WIDTH]
                acc = None
                for k in range(SLOTS):
                    e = b * SLOTS + k
                    pre = p_src[h, links[e], rows, :] + to
                    s = sigmoid(pre)
                    v = pre * s
                    acc = v if acc is None else acc + v
                    slope_edge[layer, h, e, rows, :] = (s + v * (1.0 - s)).astype(BF16)
                edge_sum[h, at, :] = acc.astype(BF16)
        total[h] = dot(edge_sum[h], w_eo[layer]).astype(BF16)
        inner = dot(total[h], w_ni[layer, WIDTH : 2 * WIDTH, :]) + p_own[h, :, WIDTH : 2 * WIDTH]
        s = sigmoid(inner)
        v = inner * s
        hidden[h] = v.astype(BF16)
        slope_node[layer, h] = s + v * (1.0 - s)
        after = x[layer, h] + dot(hidden[h], w_no[layer]).reshape(NBLK, PART, WIDTH)
        if layer + 1 < LAYERS:
            x[layer + 1, h] = after
        else:
            result[:, pl.ds(h * PART, PART), :] = after

    def flip(layer):
        flip_no[layer] = w_no[layer].T
        flip_total[layer] = w_ni[layer, WIDTH : 2 * WIDTH, :].T
        flip_eo[layer] = w_eo[layer].T
        flip_in[layer, 0:WIDTH, :] = w_ei[layer, 0:WIDTH, :].T
        flip_in[layer, WIDTH : 2 * WIDTH, :] = w_ei[layer, WIDTH : 2 * WIDTH, :].T
        flip_in[layer, 2 * WIDTH : 3 * WIDTH, :] = w_ni[layer, 0:WIDTH, :].T

    def back_far(layer, h):
        g = grad[:, pl.ds(h * PART, PART), :].reshape(ROWS, WIDTH).astype(BF16)
        d_inner = (dot(g, flip_no[layer]) * slope_node[layer, h]).astype(BF16)
        d_own[h, :, 2 * WIDTH : 3 * WIDTH] = d_inner
        d_total[h] = dot(d_inner, flip_total[layer]).astype(BF16)
        d_edge[h] = dot(d_total[h], flip_eo[layer])
        for c, rows in enumerate(chunks()):
            for b in range(NBLK):
                at = pl.ds(b * PART + c * CHUNK, CHUNK)
                up = d_edge[h, at, :]
                acc = None
                for k in range(SLOTS):
                    e = b * SLOTS + k
                    d_pre = up * slope_edge[layer, h, e, rows, :].astype(F32)
                    acc = d_pre if acc is None else acc + d_pre
                    chain[e, rows, :] = d_pre + chain[earlier[e], rows, :]
                d_own[h, at, WIDTH : 2 * WIDTH] = acc.astype(BF16)
            for b in range(NBLK):
                at = pl.ds(b * PART + c * CHUNK, CHUNK)
                d_own[h, at, 0:WIDTH] = chain[last[b], rows, :].astype(BF16)
                d_far[h, at, :] = chain[last[NBLK + b], rows, :].astype(BF16)
        d_halo = dot(d_far[h], flip_in[layer, 0:WIDTH, :]).astype(BF16)
        for d in range(4):
            back[layer, h, d] = d_halo[d * PART : (d + 1) * PART, :]

    def back_own(layer, h):
        d_normed[h] = dot(d_own[h], flip_in[layer]).reshape(NBLK, PART, WIDTH)

    def gain_terms(layer, h):
        acc = None
        for b in range(NBLK):
            for rows in chunks():
                near = d_normed[h, b, rows, :] * xhat[layer, h, b, rows, :]
                apart = back[layer, h, b, rows, :].astype(F32) * arrived[layer, h, b, rows, :].astype(F32)
                acc = near + apart if acc is None else acc + (near + apart)
        return acc

    def keep_gain(layer, acc):
        acc = jnp.sum(acc, axis=0, keepdims=True)
        for q in range(4):
            gain_mine[layer * 4 + q : layer * 4 + q + 1, :] = acc[:, q * 128 : (q + 1) * 128]

    def back_norm(layer, h):
        wait_halo(2 * LAYERS - 1 - layer, h)
        for c, rows in enumerate(chunks()):
            sent = [returned[layer, h, d, rows, :].astype(F32) for d in range(4)]
            for b in range(NBLK):
                dn = d_normed[h, b, rows, :]
                for d in range(4):
                    dn = dn + chosen[b][d] * sent[d]
                dh = dn * one_gain[layer]
                unit = xhat[layer, h, b, rows, :]
                along = jnp.mean(dh * unit, axis=-1, keepdims=True)
                r = scale[layer, h, b, rows, 0:1]
                at = pl.ds(h * PART + c * CHUNK, CHUNK)
                grad[b, at, :] = grad[b, at, :] + r * (dh - unit * along)

    for layer in range(LAYERS):
        one_gain[layer] = 1.0 + gain[layer : layer + 1, :]
    load_x[0].wait()
    norm(0, 0)
    pl.semaphore_wait(barrier, 4 + len(near) + len(far))
    send(0, 0)
    for h in range(1, STREAMS):
        load_x[h].wait()
        norm(0, h)
        send(0, h)
    for h in range(STREAMS):
        own(0, h)
    for copy in weights[0][2:] + weights[1]:
        copy.wait()
    flip(1)
    for layer in range(LAYERS):
        for h in range(STREAMS):
            finish(layer, h)
            if layer + 1 < LAYERS:
                norm(layer + 1, h)
                send(layer + 1, h)
                own(layer + 1, h)
                if h == STREAMS - 1:
                    flip(0)
            else:
                if h == 0:
                    load_g.wait()
                back_far(layer, h)
                start_halo(LAYERS, h)
                back_own(layer, h)

    for layer in reversed(range(LAYERS)):
        terms = None
        if layer == LAYERS - 1:
            for h in range(STREAMS):
                more = gain_terms(layer, h)
                terms = more if terms is None else terms + more
            keep_gain(layer, terms)
            continue
        for h in range(STREAMS):
            back_norm(layer + 1, h)
            back_far(layer, h)
            if layer > 0 or h < STREAMS - 1:
                start_halo(2 * LAYERS - 1 - layer, h)
            back_own(layer, h)
            more = gain_terms(layer, h)
            terms = more if terms is None else terms + more
        keep_gain(layer, terms)

    def near_copy(t):
        return pltpu.make_async_remote_copy(
            src_ref=gain_mine, dst_ref=gather_near.at[near_slot], send_sem=ar_send.at[0], recv_sem=ar_recv.at[0],
            device_id=near[t], device_id_type=MESH,
        )

    def far_copy(t):
        return pltpu.make_async_remote_copy(
            src_ref=gain_near, dst_ref=gather_far.at[far_slot], send_sem=ar_send.at[1], recv_sem=ar_recv.at[1],
            device_id=far[t], device_id_type=MESH,
        )

    def all_of(gather, n, sem):
        return pltpu.make_async_copy(gather.at[pl.ds(0, n)], gather.at[pl.ds(0, n)], sem)

    for t in range(len(near)):
        near_copy(t).start()
    start_halo(2 * LAYERS - 1, STREAMS - 1)
    gather_near[near_slot] = gain_mine[...]

    for h in range(STREAMS - 1):
        back_norm(0, h)
    all_of(gather_near, len(near), ar_recv.at[0]).wait()
    part = gather_near[0]
    for t in range(1, len(near) + 1):
        part = part + gather_near[t]
    gain_near[...] = part
    for t in range(len(far)):
        far_copy(t).start()
    gather_far[far_slot] = part
    back_norm(0, STREAMS - 1)
    for phase in range(2 * LAYERS):
        for h in range(STREAMS):
            for d in range(4):
                guarded((has_ahead if phase < LAYERS else has_behind)[d], halo(phase, h, d).wait_send)
    all_of(gather_near, len(near), ar_send.at[0]).wait()
    all_of(gather_far, len(far), ar_recv.at[1]).wait()
    whole = gather_far[0]
    for t in range(1, len(far) + 1):
        whole = whole + gather_far[t]
    for layer in range(LAYERS):
        for q in range(4):
            grad_gains[layer : layer + 1, q * 128 : (q + 1) * 128] = whole[layer * 4 + q : layer * 4 + q + 1, :]
    all_of(gather_far, len(far), ar_send.at[1]).wait()


def hand_over(result, grad_state, grad_gains, result_out, grad_out, gains_out, sem):
    copies = [pltpu.make_async_copy(grad_gains, gains_out, sem.at[2 * NBLK])]
    for b in range(NBLK):
        copies.append(pltpu.make_async_copy(result.at[b], result_out.at[b], sem.at[b]))
        copies.append(pltpu.make_async_copy(grad_state.at[b], grad_out.at[b], sem.at[NBLK + b]))
    for copy in copies:
        copy.start()
    for copy in copies:
        copy.wait()


def solution(mesh):
    n_lon, n_lat = mesh.shape["lon"], mesh.shape["lat"]

    def local(state, cotangent, gains, senders, halo_map, edge_in, edge_out, node_in, node_out):
        outside = pl.BlockSpec(memory_space=pltpu.HBM)
        vmem = pltpu.VMEM
        whole = (NBLK, BLOCK, WIDTH)
        split_rows = (STREAMS, NBLK, PART, WIDTH)
        flat = (STREAMS, ROWS, WIDTH)
        halos = (LAYERS, STREAMS, 4, PART, WIDTH)
        scratch = [
            vmem((LAYERS,) + split_rows, F32),
            vmem((LAYERS, WIDTH), F32),
            pltpu.SMEM((NBLK, SLOTS), jnp.int32),
            pltpu.SMEM((1, 4), jnp.int32),
            vmem((LAYERS, 2 * WIDTH, WIDTH), BF16),
            vmem((LAYERS, WIDTH, WIDTH), BF16),
            vmem((LAYERS, 2 * WIDTH, WIDTH), BF16),
            vmem((LAYERS, WIDTH, WIDTH), BF16),
            vmem((LAYERS, WIDTH, WIDTH), BF16),
            vmem((LAYERS, WIDTH, WIDTH), BF16),
            vmem((LAYERS, WIDTH, WIDTH), BF16),
            vmem((LAYERS, 3 * WIDTH, WIDTH), BF16),
            vmem((LAYERS,) + split_rows, F32),
            vmem((LAYERS, STREAMS, NBLK, PART, 128), F32),
            vmem(split_rows, BF16),
            vmem(flat, BF16),
            vmem(halos, BF16),
            vmem(halos, BF16),
            vmem(flat, BF16),
            vmem((STREAMS, 2 * NBLK, PART, WIDTH), F32),
            vmem((STREAMS, ROWS, 2 * WIDTH), F32),
            vmem((LAYERS, STREAMS, EDGES, PART, WIDTH), BF16),
            vmem((LAYERS,) + flat, F32),
            vmem(flat, BF16),
            vmem(flat, BF16),
            vmem(flat, BF16),
            vmem(flat, BF16),
            vmem(flat, F32),
            vmem((EDGES + 1, PART, WIDTH), F32),
            vmem((STREAMS, ROWS, 3 * WIDTH), BF16),
            vmem(flat, BF16),
            vmem(halos, BF16),
            vmem(halos, BF16),
            vmem(split_rows, F32),
            vmem((8, 128), F32),
            vmem((8, 128), F32),
            vmem((n_lat, 8, 128), F32),
            vmem((n_lon, 8, 128), F32),
            pltpu.SemaphoreType.DMA((4 + STREAMS,)),
            pltpu.SemaphoreType.DMA((LAYERS, 4)),
            pltpu.SemaphoreType.DMA((2 * LAYERS, STREAMS, 4)),
            pltpu.SemaphoreType.DMA((2 * LAYERS, STREAMS, 4)),
            pltpu.SemaphoreType.DMA((2,)),
            pltpu.SemaphoreType.DMA((2,)),
        ]
        result, grad_state, grad_gains = pl.pallas_call(
            lambda *refs: kernel(n_lon, n_lat, *refs),
            out_shape=(vmem(whole, F32), vmem(whole, F32), vmem((LAYERS, WIDTH), F32)),
            in_specs=[outside] * 9,
            scratch_shapes=scratch,
            compiler_params=pltpu.CompilerParams(
                collective_id=0, has_side_effects=True, vmem_limit_bytes=60 * 2**20
            ),
            cost_estimate=pl.CostEstimate(flops=4 * 10**9, bytes_accessed=10**7, transcendentals=2 * 10**6),
            name="mesh_steps",
        )(
            state.reshape(whole),
            cotangent.reshape(whole),
            gains,
            senders.reshape(NBLK, SLOTS),
            halo_map.reshape(1, 4),
            edge_in,
            edge_out,
            node_in,
            node_out,
        )
        result, grad_state, grad_gains = pl.pallas_call(
            hand_over,
            out_shape=(
                jax.ShapeDtypeStruct(whole, F32),
                jax.ShapeDtypeStruct(whole, F32),
                jax.ShapeDtypeStruct((LAYERS, WIDTH), F32),
            ),
            in_specs=[pl.BlockSpec(memory_space=pl.ANY)] * 3,
            out_specs=(outside,) * 3,
            scratch_shapes=[pltpu.SemaphoreType.DMA((2 * NBLK + 1,))],
            compiler_params=pltpu.CompilerParams(vmem_limit_bytes=2**20),
            name="hand_over",
        )(result, grad_state, grad_gains)
        shape = (1, 1, NBLK * BLOCK, WIDTH)
        return result.reshape(shape), grad_state.reshape(shape), grad_gains

    split = P("lon", "lat", None, None)
    return jax.shard_map(
        local,
        mesh=mesh,
        in_specs=(split, split, P(), split, split, P(), P(), P(), P()),
        out_specs=(split, split, P()),
        check_vma=False,
    )
```

time: 200 us -> 41.8 us (0.21)
  blocking collectives: 87.3 us -> 0 us
  Pallas kernels: 0 us -> 41.1 us
  starting transfers between devices: 39.9 us -> 0 us
  matrix products: 30.2 us -> 0 us
  other arithmetic: 23 us -> 0 us
  local copies, waits for them, and re-layouts: 12.7 us -> 0 us
  waiting for transfers between devices: 3.94 us -> 0 us
    psum x1 -> x0, blocking collectives: 87.3 us -> none  [local(): grad_gains = lax.psum(jnp.stack(gain_terms), ('lon', 'lat'))]
    pallas_call x0 -> x2, Pallas kernels: none -> 41.1 us  [the longest x1 40 us: local(): pl.pallas_call(lambda *refs: kernel(n_lon, n_lat, *refs), out_shape=(vmem...]
    ppermute x16 -> x0, starting transfers between devices: 39.9 us -> none  [the longest x8 26.4 us: padded(): lax.ppermute(tail, axis, [(i, (i + 1) % count) for i in range(ends)])]
    dot_general x24 -> x0, matrix products: 30.2 us -> none  [the longest x4 7.51 us: combine(): messages = jnp.dot(edges, second_edge, preferred_element_type=jnp.float32)]
    scatter-add x4 -> x0, other arithmetic: 8.75 us -> none  [the longest x2 7 us: combine(): jnp.take(project_src, links, axis=0).reshape(nblk, slots, block, width)]
    gather x4 -> x0, local copies, waits for them, and re-layouts: 7.07 us -> none  [the longest x2 4.05 us: combine(): jnp.take(project_src, links, axis=0).reshape(nblk, slots, block, width)]
    convert_element_type x5 -> x0, other arithmetic: 5.15 us -> none  [the longest x2 4.08 us: combine(): edges = jax.nn.silu(chosen + project_dst[:, None]).astype(jnp.bfloat16)]
    unnamed x124 -> x0, local copies, waits for them, and re-layouts: 5.07 us -> none
  transfers between devices with their start and end apart: 16 -> 0, of which waited for: 2 -> 0; matrix products, arithmetic and copies ran while one was open for 4% -> 0% of each run, Pallas kernels for 0% -> 0%
where the time goes in v3:
time: 41.8 us; the launch traced here: 41.7 us
  Pallas kernels  41.1 us (98%)
  between operations  0.64 us (2%)
    pallas_call x1, Pallas kernels, local(): pl.pallas_call(lambda *refs: kernel(n_lon, n_lat, *refs), out_shape=(vmem...  40 us
    pallas_call x1, Pallas kernels, local(): pl.pallas_call(hand_over, out_shape=(jax.ShapeDtypeStruct(whole, F32), ja...  1.04 us

profile of v3, /device:TPU:1, one launch (start us, length us, event | category | flops | bytes accessed | tf_op | source)
XLA Modules:
  0.0 41.7 jit_solution(17066707629280340660)
XLA Ops:
  0.6 40.0 %mesh_steps.1 = (f32[4,64,512]{2,1,0:T(8,128)S(1)}, f32[4,64,512]{2,1,0:T(8,128)S(1)}, f32[2,512]{1,0:T(2,128)S(1)}) custom-call(f32[4,64,512]{2,1,0:T(8,128)} %bitcast.6, f32[4,64,512]{2,1,0:T(8,128)} %bitcast.7, f32[2,512]{1,0:T(2,128)} %refs_2_.1, s32[4,4]{1,0:T(4,128)} %bitcast.10, s32[1,4]{1,0:T(1,128)} %bitcast.11, bf16[2,1024,512]{2,1,0:T(8,128)(2,1)} %refs_5_.1, ...), custom_call_target="tpu_custom_call" | custom-call | flops 4000000000 | bytes 10000000 | tf_op jit(solution)/shard_map/mesh_steps/pallas_call | solution.py:453
  40.7 1.0 %hand_over.1 = (f32[4,64,512]{2,1,0:T(8,128)}, f32[4,64,512]{2,1,0:T(8,128)}, f32[2,512]{1,0:T(2,128)}) custom-call(f32[4,64,512]{2,1,0:T(8,128)S(1)} %get-tuple-element.9.result, f32[4,64,512]{2,1,0:T(8,128)S(1)} %get-tuple-element.10.grad_state, f32[2,512]{1,0:T(2,128)S(1)} %get-tuple-element.11.grad_gains), custom_call_target="tpu_custom_call" | custom-call | tf_op jit(solution)/shard_map/hand_over/pallas_call | solution.py:474

commit v4 on v3

--- a/solution.py
+++ b/solution.py
@@ -42,10 +42,10 @@
     n_lon, n_lat,
     state, cotangent, gains, senders, picks, edge_in, edge_out, node_in, node_out,
     result, grad, grad_gains,
-    x, gain, send_ids, pick_ids, w_ei, w_eo, w_ni, w_no, flip_no, flip_total, flip_eo, flip_in,
+    x, gain, send_ids, pick_ids, w_ei, w_eo, w_ni, w_no, w_both, flip_no, flip_both, flip_in,
     xhat, scale, xhat16, normed, outgoing, arrived, normed_far, p_src, p_own,
-    slope_edge, slope_node, edge_sum, hidden, total, d_total, d_edge,
-    chain, d_own, d_far, back, returned, d_normed,
+    slope_edge, slope_node, edge_sum, hidden, d_edge,
+    chains, d_own, d_far, back, returned, d_normed,
     gain_mine, gain_near, gather_near, gather_far,
     load_sem, weight_sem, send_sem, recv_sem, ar_send, ar_recv,
 ):
@@ -107,42 +107,9 @@
         else:
             pl.when(when)(action)
 
-    zeros = jnp.zeros((PART, WIDTH), BF16)
-    for d in (2, 3):
-
-        def clear_arrived(d=d):
-            for layer in range(LAYERS):
-                for h in range(STREAMS):
-                    arrived[layer, h, d] = zeros
-
-        def clear_returned(d=d):
-            for layer in range(LAYERS):
-                for h in range(STREAMS):
-                    returned[layer, h, d] = zeros
-
-        pl.when(jnp.logical_not(has_behind[d]))(clear_arrived)
-        pl.when(jnp.logical_not(has_ahead[d]))(clear_returned)
-    chain[EDGES] = jnp.zeros((PART, WIDTH), F32)
-
     for copy in small:
         copy.wait()
     picked = [pick_ids[0, d] for d in range(4)]
-    links = [send_ids[e // SLOTS, e % SLOTS] for e in range(EDGES)]
-    chosen = [[same(picked[d], b).astype(F32) for d in range(4)] for b in range(NBLK)]
-
-    earlier = []
-    for e in range(EDGES):
-        found = jnp.int32(EDGES)
-        for f in range(e):
-            found = found + same(links[f], links[e]) * (f - found)
-        earlier.append(found)
-    last = []
-    for s in range(2 * NBLK):
-        found = jnp.int32(EDGES)
-        for f in range(EDGES):
-            found = found + same(links[f], s) * (f - found)
-        last.append(found)
-
     one_gain = [None] * LAYERS
 
     def halo(phase, h, d):
@@ -183,9 +150,6 @@
         start_halo(layer, h)
 
     def own(layer, h):
-        if layer == 0 and h == 0:
-            weights[layer][0].wait()
-            weights[layer][1].wait()
         rows = normed[h]
         p_src[h, 0:NBLK] = dot(rows, w_ei[layer, 0:WIDTH, :]).reshape(NBLK, PART, WIDTH)
         p_own[h, :, 0:WIDTH] = dot(rows, w_ei[layer, WIDTH : 2 * WIDTH, :])
@@ -211,8 +175,7 @@
                     acc = v if acc is None else acc + v
                     slope_edge[layer, h, e, rows, :] = (s + v * (1.0 - s)).astype(BF16)
                 edge_sum[h, at, :] = acc.astype(BF16)
-        total[h] = dot(edge_sum[h], w_eo[layer]).astype(BF16)
-        inner = dot(total[h], w_ni[layer, WIDTH : 2 * WIDTH, :]) + p_own[h, :, WIDTH : 2 * WIDTH]
+        inner = dot(edge_sum[h], w_both[layer]) + p_own[h, :, WIDTH : 2 * WIDTH]
         s = sigmoid(inner)
         v = inner * s
         hidden[h] = v.astype(BF16)
@@ -225,33 +188,40 @@
 
     def flip(layer):
         flip_no[layer] = w_no[layer].T
-        flip_total[layer] = w_ni[layer, WIDTH : 2 * WIDTH, :].T
-        flip_eo[layer] = w_eo[layer].T
+        flip_both[layer] = w_both[layer].T
         flip_in[layer, 0:WIDTH, :] = w_ei[layer, 0:WIDTH, :].T
         flip_in[layer, WIDTH : 2 * WIDTH, :] = w_ei[layer, WIDTH : 2 * WIDTH, :].T
         flip_in[layer, 2 * WIDTH : 3 * WIDTH, :] = w_ni[layer, 0:WIDTH, :].T
+
+    def pieces():
+        return [
+            (chains[2 * c + half], rows, pl.ds(half * (WIDTH // 2), WIDTH // 2))
+            for c, rows in enumerate(chunks())
+            for half in range(2)
+        ]
 
     def back_far(layer, h):
         g = grad[:, pl.ds(h * PART, PART), :].reshape(ROWS, WIDTH).astype(BF16)
         d_inner = (dot(g, flip_no[layer]) * slope_node[layer, h]).astype(BF16)
         d_own[h, :, 2 * WIDTH : 3 * WIDTH] = d_inner
-        d_total[h] = dot(d_inner, flip_total[layer]).astype(BF16)
-        d_edge[h] = dot(d_total[h], flip_eo[layer])
-        for c, rows in enumerate(chunks()):
-            for b in range(NBLK):
-                at = pl.ds(b * PART + c * CHUNK, CHUNK)
-                up = d_edge[h, at, :]
-                acc = None
-                for k in range(SLOTS):
-                    e = b * SLOTS + k
-                    d_pre = up * slope_edge[layer, h, e, rows, :].astype(F32)
-                    acc = d_pre if acc is None else acc + d_pre
-                    chain[e, rows, :] = d_pre + chain[earlier[e], rows, :]
-                d_own[h, at, WIDTH : 2 * WIDTH] = acc.astype(BF16)
-            for b in range(NBLK):
-                at = pl.ds(b * PART + c * CHUNK, CHUNK)
-                d_own[h, at, 0:WIDTH] = chain[last[b], rows, :].astype(BF16)
-                d_far[h, at, :] = chain[last[NBLK + b], rows, :].astype(BF16)
+        d_edge[h] = dot(d_inner, flip_both[layer])
+        for b in range(NBLK):
+            acc = [None] * len(chains)
+            for k in range(SLOTS):
+                e = b * SLOTS + k
+                for q, (chain, rows, cols) in enumerate(pieces()):
+                    at = pl.ds(b * PART + rows.start, CHUNK)
+                    d_pre = d_edge[h, at, cols] * slope_edge[layer, h, e, rows, cols].astype(F32)
+                    acc[q] = d_pre if k == 0 else acc[q] + d_pre
+                    chain[e] = d_pre + chain[earlier[e]]
+            for q, (chain, rows, cols) in enumerate(pieces()):
+                at = pl.ds(b * PART + rows.start, CHUNK)
+                d_own[h, at, pl.ds(WIDTH + cols.start, cols.size)] = acc[q].astype(BF16)
+        for b in range(NBLK):
+            for chain, rows, cols in pieces():
+                at = pl.ds(b * PART + rows.start, CHUNK)
+                d_far[h, at, cols] = chain[last[NBLK + b]].astype(BF16)
+                d_own[h, at, cols] = chain[last[b]].astype(BF16)
         d_halo = dot(d_far[h], flip_in[layer, 0:WIDTH, :]).astype(BF16)
         for d in range(4):
             back[layer, h, d] = d_halo[d * PART : (d + 1) * PART, :]
@@ -298,31 +268,70 @@
         load_x[h].wait()
         norm(0, h)
         send(0, h)
+    for copy in weights[0][:2]:
+        copy.wait()
     for h in range(STREAMS):
         own(0, h)
+
+    zeros = jnp.zeros((PART, WIDTH), BF16)
+    for d in (2, 3):
+
+        def clear_arrived(d=d):
+            for layer in range(LAYERS):
+                for h in range(STREAMS):
+                    arrived[layer, h, d] = zeros
+
+        def clear_returned(d=d):
+            for layer in range(LAYERS):
+                for h in range(STREAMS):
+                    returned[layer, h, d] = zeros
+
+        pl.when(jnp.logical_not(has_behind[d]))(clear_arrived)
+        pl.when(jnp.logical_not(has_ahead[d]))(clear_returned)
+    for chain in chains:
+        chain[EDGES] = jnp.zeros((CHUNK, WIDTH // 2), F32)
+
+    links = [send_ids[e // SLOTS, e % SLOTS] for e in range(EDGES)]
+    chosen = [[same(picked[d], b).astype(F32) for d in range(4)] for b in range(NBLK)]
+
+    earlier = []
+    for e in range(EDGES):
+        found = jnp.int32(EDGES)
+        for f in range(e):
+            found = found + same(links[f], links[e]) * (f - found)
+        earlier.append(found)
+    last = []
+    for s in range(2 * NBLK):
+        found = jnp.int32(EDGES)
+        for f in range(EDGES):
+            found = found + same(links[f], s) * (f - found)
+        last.append(found)
+
     for copy in weights[0][2:] + weights[1]:
         copy.wait()
+    for layer in range(LAYERS):
+        w_both[layer] = dot(w_eo[layer], w_ni[layer, WIDTH : 2 * WIDTH, :]).astype(BF16)
     flip(1)
-    for layer in range(LAYERS):
+
+    for layer in range(LAYERS - 1):
         for h in range(STREAMS):
             finish(layer, h)
-            if layer + 1 < LAYERS:
-                norm(layer + 1, h)
-                send(layer + 1, h)
-                own(layer + 1, h)
-                if h == STREAMS - 1:
-                    flip(0)
-            else:
-                if h == 0:
-                    load_g.wait()
-                back_far(layer, h)
-                start_halo(LAYERS, h)
-                back_own(layer, h)
+            norm(layer + 1, h)
+            send(layer + 1, h)
+        for h in range(STREAMS):
+            own(layer + 1, h)
+        flip(layer)
+    load_g.wait()
+    for h in range(STREAMS):
+        finish(LAYERS - 1, h)
+        back_far(LAYERS - 1, h)
+        start_halo(LAYERS, h)
 
     for layer in reversed(range(LAYERS)):
         terms = None
         if layer == LAYERS - 1:
             for h in range(STREAMS):
+                back_own(layer, h)
                 more = gain_terms(layer, h)
                 terms = more if terms is None else terms + more
             keep_gain(layer, terms)
@@ -430,10 +439,8 @@
             vmem((LAYERS,) + flat, F32),
             vmem(flat, BF16),
             vmem(flat, BF16),
-            vmem(flat, BF16),
-            vmem(flat, BF16),
             vmem(flat, F32),
-            vmem((EDGES + 1, PART, WIDTH), F32),
+            [vmem((EDGES + 1, CHUNK, WIDTH // 2), F32)] * (2 * (PART // CHUNK)),
             vmem((STREAMS, ROWS, 3 * WIDTH), BF16),
             vmem(flat, BF16),
             vmem(halos, BF16),

time: 41.8 us -> 40 us (0.957)
  Pallas kernels: 41.1 us -> 39.3 us
    pallas_call x1, Pallas kernels: 40 us -> 38.2 us  [local(): pl.pallas_call(lambda *refs: kernel(n_lon, n_lat, *refs), out_shape=(vmem...]
where the time goes in v4:
time: 40 us; the launch traced here: 39.9 us
  Pallas kernels  39.3 us (98%)
  between operations  0.64 us (2%)
    pallas_call x1, Pallas kernels, local(): pl.pallas_call(lambda *refs: kernel(n_lon, n_lat, *refs), out_shape=(vmem...  38.2 us
    pallas_call x1, Pallas kernels, local(): pl.pallas_call(hand_over, out_shape=(jax.ShapeDtypeStruct(whole, F32), ja...  1.04 us

profile of v4, /device:TPU:1, one launch (start us, length us, event | category | flops | bytes accessed | tf_op | source)
XLA Modules:
  0.0 39.9 jit_solution(11650607666424947518)
XLA Ops:
  0.6 38.2 %mesh_steps.1 = (f32[4,64,512]{2,1,0:T(8,128)S(1)}, f32[4,64,512]{2,1,0:T(8,128)S(1)}, f32[2,512]{1,0:T(2,128)S(1)}) custom-call(f32[4,64,512]{2,1,0:T(8,128)} %bitcast.6, f32[4,64,512]{2,1,0:T(8,128)} %bitcast.7, f32[2,512]{1,0:T(2,128)} %refs_2_.1, s32[4,4]{1,0:T(4,128)} %bitcast.10, s32[1,4]{1,0:T(1,128)} %bitcast.11, bf16[2,1024,512]{2,1,0:T(8,128)(2,1)} %refs_5_.1, ...), custom_call_target="tpu_custom_call" | custom-call | flops 4000000000 | bytes 10000000 | tf_op jit(solution)/shard_map/mesh_steps/pallas_call | solution.py:460
  38.9 1.0 %hand_over.1 = (f32[4,64,512]{2,1,0:T(8,128)}, f32[4,64,512]{2,1,0:T(8,128)}, f32[2,512]{1,0:T(2,128)}) custom-call(f32[4,64,512]{2,1,0:T(8,128)S(1)} %get-tuple-element.9.result, f32[4,64,512]{2,1,0:T(8,128)S(1)} %get-tuple-element.10.grad_state, f32[2,512]{1,0:T(2,128)S(1)} %get-tuple-element.11.grad_gains), custom_call_target="tpu_custom_call" | custom-call | tf_op jit(solution)/shard_map/hand_over/pallas_call | solution.py:481

commit v5 on v4

--- a/solution.py
+++ b/solution.py
@@ -30,8 +30,10 @@
     return 1 - jnp.minimum(apart * apart, 1)
 
 
-def sigmoid(v):
-    return 0.5 * jnp.tanh(0.5 * v) + 0.5
+def silu_of_half(v):
+    u = 1.0 + jnp.tanh(v)
+    out = v * u
+    return out, u + out * (2.0 - u)
 
 
 def chunks():
@@ -44,7 +46,7 @@
     result, grad, grad_gains,
     x, gain, send_ids, pick_ids, w_ei, w_eo, w_ni, w_no, w_both, flip_no, flip_both, flip_in,
     xhat, scale, xhat16, normed, outgoing, arrived, normed_far, p_src, p_own,
-    slope_edge, slope_node, edge_sum, hidden, d_edge,
+    slope_edge, slope_node, edge_sum, hidden, d_hidden, d_edge,
     chains, d_own, d_far, back, returned, d_normed,
     gain_mine, gain_near, gather_near, gather_far,
     load_sem, weight_sem, send_sem, recv_sem, ar_send, ar_recv,
@@ -151,9 +153,9 @@
 
     def own(layer, h):
         rows = normed[h]
-        p_src[h, 0:NBLK] = dot(rows, w_ei[layer, 0:WIDTH, :]).reshape(NBLK, PART, WIDTH)
-        p_own[h, :, 0:WIDTH] = dot(rows, w_ei[layer, WIDTH : 2 * WIDTH, :])
-        p_own[h, :, WIDTH : 2 * WIDTH] = dot(rows, w_ni[layer, 0:WIDTH, :])
+        p_src[h, 0:NBLK] = (0.5 * dot(rows, w_ei[layer, 0:WIDTH, :])).reshape(NBLK, PART, WIDTH)
+        p_own[h, :, 0:WIDTH] = 0.5 * dot(rows, w_ei[layer, WIDTH : 2 * WIDTH, :])
+        p_own[h, :, WIDTH : 2 * WIDTH] = 0.5 * dot(rows, w_ni[layer, 0:WIDTH, :])
 
     def finish(layer, h):
         wait_halo(layer, h)
@@ -161,7 +163,7 @@
             normed_far[h, d * PART : (d + 1) * PART, :] = (
                 arrived[layer, h, d].astype(F32) * one_gain[layer]
             ).astype(BF16)
-        p_src[h, NBLK : 2 * NBLK] = dot(normed_far[h], w_ei[layer, 0:WIDTH, :]).reshape(NBLK, PART, WIDTH)
+        p_src[h, NBLK : 2 * NBLK] = (0.5 * dot(normed_far[h], w_ei[layer, 0:WIDTH, :])).reshape(NBLK, PART, WIDTH)
         for c, rows in enumerate(chunks()):
             for b in range(NBLK):
                 at = pl.ds(b * PART + c * CHUNK, CHUNK)
@@ -169,17 +171,16 @@
                 acc = None
                 for k in range(SLOTS):
                     e = b * SLOTS + k
-                    pre = p_src[h, links[e], rows, :] + to
-                    s = sigmoid(pre)
-                    v = pre * s
+                    v, slope = silu_of_half(p_src[h, links[e], rows, :] + to)
                     acc = v if acc is None else acc + v
-                    slope_edge[layer, h, e, rows, :] = (s + v * (1.0 - s)).astype(BF16)
+                    slope_edge[layer, h, e, rows, :] = slope
                 edge_sum[h, at, :] = acc.astype(BF16)
-        inner = dot(edge_sum[h], w_both[layer]) + p_own[h, :, WIDTH : 2 * WIDTH]
-        s = sigmoid(inner)
-        v = inner * s
+        inner = 0.5 * dot(edge_sum[h], w_both[layer]) + p_own[h, :, WIDTH : 2 * WIDTH]
+        v, slope = silu_of_half(inner)
         hidden[h] = v.astype(BF16)
-        slope_node[layer, h] = s + v * (1.0 - s)
+        slope_node[layer, h] = 0.5 * slope
+
+    def close(layer, h):
         after = x[layer, h] + dot(hidden[h], w_no[layer]).reshape(NBLK, PART, WIDTH)
         if layer + 1 < LAYERS:
             x[layer + 1, h] = after
@@ -200,18 +201,23 @@
             for half in range(2)
         ]
 
+    def back_hidden(layer, h):
+        g = grad[:, pl.ds(h * PART, PART), :].reshape(ROWS, WIDTH).astype(BF16)
+        d_hidden[h] = dot(g, flip_no[layer])
+
     def back_far(layer, h):
-        g = grad[:, pl.ds(h * PART, PART), :].reshape(ROWS, WIDTH).astype(BF16)
-        d_inner = (dot(g, flip_no[layer]) * slope_node[layer, h]).astype(BF16)
-        d_own[h, :, 2 * WIDTH : 3 * WIDTH] = d_inner
-        d_edge[h] = dot(d_inner, flip_both[layer])
+        if layer < LAYERS - 1:
+            back_hidden(layer, h)
+        d_inner = (d_hidden[h] * slope_node[layer, h]).astype(BF16)
+        d_edge[h] = 0.5 * dot(d_inner, flip_both[layer])
+        d_normed[h] = dot(d_inner, flip_in[layer, 2 * WIDTH : 3 * WIDTH, :]).reshape(NBLK, PART, WIDTH)
         for b in range(NBLK):
             acc = [None] * len(chains)
             for k in range(SLOTS):
                 e = b * SLOTS + k
                 for q, (chain, rows, cols) in enumerate(pieces()):
                     at = pl.ds(b * PART + rows.start, CHUNK)
-                    d_pre = d_edge[h, at, cols] * slope_edge[layer, h, e, rows, cols].astype(F32)
+                    d_pre = d_edge[h, at, cols] * slope_edge[layer, h, e, rows, cols]
                     acc[q] = d_pre if k == 0 else acc[q] + d_pre
                     chain[e] = d_pre + chain[earlier[e]]
             for q, (chain, rows, cols) in enumerate(pieces()):
@@ -227,7 +233,8 @@
             back[layer, h, d] = d_halo[d * PART : (d + 1) * PART, :]
 
     def back_own(layer, h):
-        d_normed[h] = dot(d_own[h], flip_in[layer]).reshape(NBLK, PART, WIDTH)
+        more = dot(d_own[h], flip_in[layer, 0 : 2 * WIDTH, :]).reshape(NBLK, PART, WIDTH)
+        d_normed[h] = d_normed[h] + more
 
     def gain_terms(layer, h):
         acc = None
@@ -316,6 +323,7 @@
     for layer in range(LAYERS - 1):
         for h in range(STREAMS):
             finish(layer, h)
+            close(layer, h)
             norm(layer + 1, h)
             send(layer + 1, h)
         for h in range(STREAMS):
@@ -323,6 +331,8 @@
         flip(layer)
     load_g.wait()
     for h in range(STREAMS):
+        back_hidden(LAYERS - 1, h)
+    for h in range(STREAMS):
         finish(LAYERS - 1, h)
         back_far(LAYERS - 1, h)
         start_halo(LAYERS, h)
@@ -331,6 +341,7 @@
         terms = None
         if layer == LAYERS - 1:
             for h in range(STREAMS):
+                close(layer, h)
                 back_own(layer, h)
                 more = gain_terms(layer, h)
                 terms = more if terms is None else terms + more
@@ -435,13 +446,14 @@
             vmem(flat, BF16),
             vmem((STREAMS, 2 * NBLK, PART, WIDTH), F32),
             vmem((STREAMS, ROWS, 2 * WIDTH), F32),
-            vmem((LAYERS, STREAMS, EDGES, PART, WIDTH), BF16),
+            vmem((LAYERS, STREAMS, EDGES, PART, WIDTH), F32),
             vmem((LAYERS,) + flat, F32),
             vmem(flat, BF16),
             vmem(flat, BF16),
             vmem(flat, F32),
+            vmem(flat, F32),
             [vmem((EDGES + 1, CHUNK, WIDTH // 2), F32)] * (2 * (PART // CHUNK)),
-            vmem((STREAMS, ROWS, 3 * WIDTH), BF16),
+            vmem((STREAMS, ROWS, 2 * WIDTH), BF16),
             vmem(flat, BF16),
             vmem(halos, BF16),
             vmem(halos, BF16),

time: 40 us -> 39.3 us (0.982)
  Pallas kernels: 39.3 us -> 38.5 us
    pallas_call x1, Pallas kernels: 38.2 us -> 37.5 us  [local(): pl.pallas_call(lambda *refs: kernel(n_lon, n_lat, *refs), out_shape=(vmem...]
where the time goes in v5:
time: 39.3 us; the launch traced here: 39.2 us
  Pallas kernels  38.5 us (98%)
  between operations  0.64 us (2%)
    pallas_call x1, Pallas kernels, local(): pl.pallas_call(lambda *refs: kernel(n_lon, n_lat, *refs), out_shape=(vmem...  37.5 us
    pallas_call x1, Pallas kernels, local(): pl.pallas_call(hand_over, out_shape=(jax.ShapeDtypeStruct(whole, F32), ja...  1.04 us

profile of v5, /device:TPU:1, one launch (start us, length us, event | category | flops | bytes accessed | tf_op | source)
XLA Modules:
  0.0 39.2 jit_solution(17169024834639182138)
XLA Ops:
  0.6 37.5 %mesh_steps.1 = (f32[4,64,512]{2,1,0:T(8,128)S(1)}, f32[4,64,512]{2,1,0:T(8,128)S(1)}, f32[2,512]{1,0:T(2,128)S(1)}) custom-call(f32[4,64,512]{2,1,0:T(8,128)} %bitcast.6, f32[4,64,512]{2,1,0:T(8,128)} %bitcast.7, f32[2,512]{1,0:T(2,128)} %refs_2_.1, s32[4,4]{1,0:T(4,128)} %bitcast.10, s32[1,4]{1,0:T(1,128)} %bitcast.11, bf16[2,1024,512]{2,1,0:T(8,128)(2,1)} %refs_5_.1, ...), custom_call_target="tpu_custom_call" | custom-call | flops 4000000000 | bytes 10000000 | tf_op jit(solution)/shard_map/mesh_steps/pallas_call | solution.py:472
  38.1 1.0 %hand_over.1 = (f32[4,64,512]{2,1,0:T(8,128)}, f32[4,64,512]{2,1,0:T(8,128)}, f32[2,512]{1,0:T(2,128)}) custom-call(f32[4,64,512]{2,1,0:T(8,128)S(1)} %get-tuple-element.9.result, f32[4,64,512]{2,1,0:T(8,128)S(1)} %get-tuple-element.10.grad_state, f32[2,512]{1,0:T(2,128)S(1)} %get-tuple-element.11.grad_gains), custom_call_target="tpu_custom_call" | custom-call | tf_op jit(solution)/shard_map/hand_over/pallas_call | solution.py:493

commit v6 on v5

--- a/solution.py
+++ b/solution.py
@@ -49,7 +49,7 @@
     slope_edge, slope_node, edge_sum, hidden, d_hidden, d_edge,
     chains, d_own, d_far, back, returned, d_normed,
     gain_mine, gain_near, gather_near, gather_far,
-    load_sem, weight_sem, send_sem, recv_sem, ar_send, ar_recv,
+    load_sem, weight_sem, send_sem, recv_sem, ar_send, ar_recv, heard, heard_across,
 ):
     i = lax.axis_index("lon")
     j = lax.axis_index("lat")
@@ -96,7 +96,7 @@
         ((column + t) % columns * 2 + core, (high + c) % 2 * depth + z)
         for c in (1, 0) for t in sorted(range(columns), key=lambda t: -apart(t, columns)) if c + t > 0
     ]
-    for device in ahead + tuple(near) + tuple(far):
+    for device in ahead:
         pl.semaphore_signal(barrier, inc=1, device_id=device, device_id_type=MESH)
     for layer in range(LAYERS):
         for copy in weights[layer]:
@@ -265,11 +265,33 @@
                 at = pl.ds(h * PART + c * CHUNK, CHUNK)
                 grad[b, at, :] = grad[b, at, :] + r * (dh - unit * along)
 
+    steps = (2, 4)
+
+    def tell(r):
+        step = steps[r]
+        if step % n_lon:
+            for d, to in ((0, lax.rem(i + step, n_lon)), (1, lax.rem(i + n_lon - step % n_lon, n_lon))):
+                pl.semaphore_signal(heard.at[r, d], inc=1, device_id=(to, j), device_id_type=MESH)
+        for d, to, there in ((2, j + step, j + step < n_lat), (3, j - step, j >= step)):
+
+            def say(d=d, to=to):
+                pl.semaphore_signal(heard.at[r, d], inc=1, device_id=(i, to), device_id_type=MESH)
+
+            pl.when(there)(say)
+
+    def hear(r):
+        step = steps[r]
+        if step % n_lon:
+            for d in (0, 1):
+                pl.semaphore_wait(heard.at[r, d], 1)
+        for d, there in ((2, j >= step), (3, j + step < n_lat)):
+            pl.when(there)(lambda d=d: pl.semaphore_wait(heard.at[r, d], 1))
+
     for layer in range(LAYERS):
         one_gain[layer] = 1.0 + gain[layer : layer + 1, :]
     load_x[0].wait()
     norm(0, 0)
-    pl.semaphore_wait(barrier, 4 + len(near) + len(far))
+    pl.semaphore_wait(barrier, 4)
     send(0, 0)
     for h in range(1, STREAMS):
         load_x[h].wait()
@@ -326,6 +348,8 @@
             close(layer, h)
             norm(layer + 1, h)
             send(layer + 1, h)
+            if layer == 0 and h == 0:
+                tell(0)
         for h in range(STREAMS):
             own(layer + 1, h)
         flip(layer)
@@ -336,6 +360,9 @@
         finish(LAYERS - 1, h)
         back_far(LAYERS - 1, h)
         start_halo(LAYERS, h)
+        if h == 0:
+            hear(0)
+            tell(1)
 
     for layer in reversed(range(LAYERS)):
         terms = None
@@ -352,6 +379,11 @@
             back_far(layer, h)
             if layer > 0 or h < STREAMS - 1:
                 start_halo(2 * LAYERS - 1 - layer, h)
+            if layer == 0 and h == 0:
+                hear(1)
+                pl.semaphore_signal(
+                    heard_across, inc=1, device_id=(i, lax.rem(j + depth, n_lat)), device_id_type=MESH
+                )
             back_own(layer, h)
             more = gain_terms(layer, h)
             terms = more if terms is None else terms + more
@@ -384,6 +416,7 @@
     for t in range(1, len(near) + 1):
         part = part + gather_near[t]
     gain_near[...] = part
+    pl.semaphore_wait(heard_across, 1)
     for t in range(len(far)):
         far_copy(t).start()
     gather_far[far_slot] = part
@@ -468,6 +501,8 @@
             pltpu.SemaphoreType.DMA((2 * LAYERS, STREAMS, 4)),
             pltpu.SemaphoreType.DMA((2,)),
             pltpu.SemaphoreType.DMA((2,)),
+            pltpu.SemaphoreType.REGULAR((2, 4)),
+            pltpu.SemaphoreType.REGULAR,
         ]
         result, grad_state, grad_gains = pl.pallas_call(
             lambda *refs: kernel(n_lon, n_lat, *refs),

time: 39.3 us -> 38.5 us (0.980)
  Pallas kernels: 38.5 us -> 37.7 us
    pallas_call x1, Pallas kernels: 37.5 us -> 36.7 us  [local(): pl.pallas_call(lambda *refs: kernel(n_lon, n_lat, *refs), out_shape=(vmem...]
where the time goes in v6:
time: 38.5 us; the launch traced here: 38.4 us
  Pallas kernels  37.7 us (98%)
  between operations  0.64 us (2%)
    pallas_call x1, Pallas kernels, local(): pl.pallas_call(lambda *refs: kernel(n_lon, n_lat, *refs), out_shape=(vmem...  36.7 us
    pallas_call x1, Pallas kernels, local(): pl.pallas_call(hand_over, out_shape=(jax.ShapeDtypeStruct(whole, F32), ja...  1.04 us

profile of v6, /device:TPU:1, one launch (start us, length us, event | category | flops | bytes accessed | tf_op | source)
XLA Modules:
  0.0 38.4 jit_solution(4552408314416353429)
XLA Ops:
  0.6 36.7 %mesh_steps.1 = (f32[4,64,512]{2,1,0:T(8,128)S(1)}, f32[4,64,512]{2,1,0:T(8,128)S(1)}, f32[2,512]{1,0:T(2,128)S(1)}) custom-call(f32[4,64,512]{2,1,0:T(8,128)} %bitcast.6, f32[4,64,512]{2,1,0:T(8,128)} %bitcast.7, f32[2,512]{1,0:T(2,128)} %refs_2_.1, s32[4,4]{1,0:T(4,128)} %bitcast.10, s32[1,4]{1,0:T(1,128)} %bitcast.11, bf16[2,1024,512]{2,1,0:T(8,128)(2,1)} %refs_5_.1, ...), custom_call_target="tpu_custom_call" | custom-call | flops 4000000000 | bytes 10000000 | tf_op jit(solution)/shard_map/mesh_steps/pallas_call | solution.py:507
  37.3 1.0 %hand_over.1 = (f32[4,64,512]{2,1,0:T(8,128)}, f32[4,64,512]{2,1,0:T(8,128)}, f32[2,512]{1,0:T(2,128)}) custom-call(f32[4,64,512]{2,1,0:T(8,128)S(1)} %get-tuple-element.9.result, f32[4,64,512]{2,1,0:T(8,128)S(1)} %get-tuple-element.10.grad_state, f32[2,512]{1,0:T(2,128)S(1)} %get-tuple-element.11.grad_gains), custom_call_target="tpu_custom_call" | custom-call | tf_op jit(solution)/shard_map/hand_over/pallas_call | solution.py:528
